TPU v7x, 128 devices: a whole 4x4x4 slice. The times are simulated.
128 devices in a mesh: leaf: 4 (over x), col: 32 (over z, y, core).
Axes of the slice: x: 4, y: 4, z: 4, core: 2. Of those that a mesh axis runs over, the one named last changes fastest.
Arguments:
- incident: float32 [3072, 16384], P('leaf', 'col'), may hold values from -6 to 6
- sources: float32 [3072, 16384], P('leaf', 'col'), may hold values from -6 to 6
- tree_order: int32 [4, 768], P('leaf'), may hold values from 0 to 767, each once within a row
- near_quad: float32 [4096, 768], P('leaf'), may hold values from -0.21875 to 0.21875
- near_owner: int32 [4096, 1], P('leaf'), may hold values from 0 to 3; in each aligned block of 1024 rows (0 to 1023, 1024 to 2047, ...) at most 512 rows name the same one
- near_slot: int32 [4096], P('leaf'), may hold values from 0 to 767
- leaf_inverse: float32 [3072, 768], P(('leaf', 'col')), may hold values from -0.21875 to 0.21875
- basis_v: float32 [2, 3072, 128], P(None, ('leaf', 'col')), may hold values from -6 to 6
- basis_w: float32 [2, 2, 3072, 128], P(None, None, ('leaf', 'col')), may hold values from -0.125 to 0.125
Outputs:
- solution: float32 [3072, 16384], P('leaf', 'col')
Inputs may be any that keep to these rules, and one draw needn't show every extreme that they name: `near_owner`: in the rows of one leaf block (aligned blocks of 1024 rows), no owner is named by more than 512 rows, a bound that some block reaches. Each row of tree_order names every number once.
All inputs are finite; a program needn't handle non-finite values.
Results may differ from a plain program's by a relative error of at most 0.0001.
Values sent between devices are 32-bit elements; how exact they have to be, the bound alone decides.
A program may use at most 192 MiB of HBM per device.

v0:
```python
import math

import jax
import jax.numpy as jnp
from jax import lax
from jax.sharding import PartitionSpec as P


def partner(value, axis, distance):
    return lax.ppermute(value, axis, [(i, i ^ 1 << distance) for i in range(lax.axis_size(axis))])


def child_total(coeff, level):
    total = coeff
    for bit in range(level - 1):
        total = total + partner(total, "leaf", bit)
    return total


def sibling_of(total, level):
    return partner(total, "leaf", level - 1)


def per_device(
    incident, sources, tree_order, near_quad, near_owner, near_slot, leaf_inverse, basis_v, basis_w
):
    high = lax.Precision.HIGHEST
    leaf_rows = incident.shape[0]
    rhs_local = incident.shape[1]
    near_rows = near_quad.shape[0]
    leaf_count = lax.axis_size("leaf")
    levels = leaf_count.bit_length() - 1
    capacity = max(2, 2 * near_rows // leaf_count)
    partial_value = jnp.dot(near_quad, sources, precision=high, preferred_element_type=jnp.float32)
    owners = near_owner[:, 0]
    onehot = (owners[:, None] == jnp.arange(leaf_count, dtype=jnp.int32)[None, :]).astype(jnp.int32)
    before = jnp.cumsum(onehot, axis=0) - onehot
    placing = owners * capacity + jnp.sum(before * onehot, axis=1)
    bucket_vals = (
        jnp.zeros((leaf_count * capacity, rhs_local), jnp.float32).at[placing].set(partial_value)
    )
    bucket_slots = (
        jnp.zeros((leaf_count * capacity,), jnp.float32)
        .at[placing]
        .set(near_slot.astype(jnp.float32))
    )
    arrived_vals, arrived_slots = (
        lax.all_to_all(bucket_vals, "leaf", split_axis=0, concat_axis=0, tiled=True),
        lax.all_to_all(bucket_slots, "leaf", split_axis=0, concat_axis=0, tiled=True),
    )
    assembled = incident.at[arrived_slots.astype(jnp.int32)].add(arrived_vals)
    order_row = tree_order[0]
    ordered = assembled[order_row]
    state = jnp.dot(
        lax.all_gather(leaf_inverse, "col", axis=0, tiled=True),
        ordered,
        precision=high,
        preferred_element_type=jnp.float32,
    )
    contract = (((0,), (0,)), ((), ()))
    merged_w = basis_w.reshape(levels * 2, basis_w.shape[2], basis_w.shape[3])
    full_v, full_w = (
        lax.all_gather(basis_v, "col", axis=1, tiled=True),
        lax.all_gather(merged_w, "col", axis=1, tiled=True),
    )
    full_w = full_w.reshape(levels, 2, leaf_rows, full_w.shape[2])
    for level in range(1, levels + 1):
        scale = 1.0 / math.sqrt(2 ** (level - 1) * leaf_rows)
        coeff = (
            lax.dot_general(
                full_v[level - 1],
                state,
                contract,
                precision=high,
                preferred_element_type=jnp.float32,
            )
            * scale
        )
        own_sum = child_total(coeff, level)
        sibling = sibling_of(own_sum, level)
        update = jnp.dot(
            full_w[level - 1, 0], sibling, precision=high, preferred_element_type=jnp.float32
        ) + jnp.dot(
            full_w[level - 1, 1], own_sum, precision=high, preferred_element_type=jnp.float32
        )
        state = state - update
    solution = jnp.zeros((leaf_rows, rhs_local), jnp.float32).at[order_row].set(state)
    return solution


def solution(mesh):
    placed = (
        P("leaf", "col"),
        P("leaf", "col"),
        P("leaf", None),
        P("leaf", None),
        P("leaf", None),
        P("leaf"),
        P(("leaf", "col"), None),
        P(None, ("leaf", "col"), None),
        P(None, None, ("leaf", "col"), None),
    )
    return jax.shard_map(
        per_device, mesh=mesh, in_specs=placed, out_specs=P("leaf", "col"), check_vma=False
    )
```

profile of v0, /device:TPU:0, one launch (start us, length us, event | category | flops | bytes accessed | tf_op | source)
XLA Modules:
  0.0 170.4 jit_solution(7152544434941609103)
XLA Ops:
  6.5 0.0 copy-start
  6.5 0.0 copy-start.6
  6.5 0.0 copy-start.8
  6.5 0.0 all-gather.3.cloned.1.call-start
  6.5 2.8 %copy.18 = f32[768,512]{1,0:T(8,128)} copy(f32[768,512]{1,0:T(8,128)} %param.9) | data formatting | bytes 3145728
  9.4 0.0 all-gather.3.cloned.1.call-update
  9.4 0.0 copy-done.6
  9.4 1.1 reduce-window.6
  10.6 0.2 slice_reduce_fusion
  10.8 0.2 reduce-window.9
  11.0 0.0 copy-done.8
  11.0 0.1 add_bitcast_fusion
  11.1 4.9 %scatter_custom_fusion = f32[2048]{0:T(1024)} fusion(s32[1024]{0:T(1024)S(1)} %bitcast.78, f32[1024]{0:T(1024)S(1)} %convert_element_type.25, f32[]{:T(128)} %constant.7.clone.1), kind=kCustom, calls=%fused_computation.35 | custom fusion | bytes 8196 | tf_op jit(solution)/shard_map/scatter | solution.py:45
  16.0 4.4 %all-to-all-start = ((f32[4,512,1]{1,2,0:T(1,128)}), f32[4,512,1]{1,2,0:T(1,128)S(1)}, u32[]{:S(2)}, u32[]{:S(2)}) async-start(f32[4,512,1]{1,2,0:T(1,128)} %bitcast.6), calls=%async_computation | async-start | bytes 16384 | tf_op jit(solution)/shard_map/all_to_all | solution.py:49
  20.3 0.0 copy-done
  20.4 7.8 %fusion.14 = f32[1024,512]{1,0:T(8,128)} fusion(f32[1024,768]{1,0:T(8,128)S(1)} %copy-done, f32[768,512]{1,0:T(8,128)} %param.10), kind=kOutput, calls=%fused_computation.38 | convolution fusion | flops 4831838208 | bytes 6815744 | tf_op jit(solution)/shard_map/dot_general | solution.py:34
  28.2 7.6 %scatter_custom_fusion.1 = f32[2048,512]{1,0:T(8,128)} fusion(s32[1024]{0:T(1024)S(1)} %bitcast.79, f32[1024,512]{1,0:T(8,128)} %fusion.14, f32[]{:T(128)} %constant.7.clone.1), kind=kCustom, calls=%fused_computation.5 | custom fusion | bytes 4194816 | tf_op jit(solution)/shard_map/scatter | solution.py:40
  35.8 0.0 all-to-all-done
  35.8 0.0 copy-start.9
  35.8 0.0 copy-start.7
  35.8 5.0 %all-to-all-start.1 = ((f32[4,512,512]{2,1,0:T(8,128)}), f32[4,512,512]{2,1,0:T(8,128)}, u32[]{:S(2)}, u32[]{:S(2)}) async-start(f32[4,512,512]{2,1,0:T(8,128)} %bitcast.65), calls=%async_computation.1 | async-start | bytes 8388608 | tf_op jit(solution)/shard_map/all_to_all | solution.py:48
  40.8 0.0 all-gather.5.cloned.1.call-start
  40.8 0.7 all-gather.5.cloned.1.call-update
  41.5 0.0 copy-done.9
  41.6 0.0 copy-done.7
  41.6 28.9 %all_gather.10 = f32[2,768,128]{2,1,0:T(8,128)} all-gather(f32[2,24,128]{2,1,0:T(8,128)S(1)} %copy-done.7), channel_id=1, replica_groups=mesh['leaf'=4,'col'=32] {'col'}, dimensions={1}, use_global_device_ids=true | all-gather | bytes 811008 | tf_op jit(solution)/shard_map/all_gather | solution.py:63
  70.5 19.2 %all-to-all-done.1 = f32[4,512,512]{2,1,0:T(8,128)} async-done(((f32[4,512,512]{2,1,0:T(8,128)}), f32[4,512,512]{2,1,0:T(8,128)}, u32[]{:S(2)}, u32[]{:S(2)}) %all-to-all-start.1) | async-done | bytes 4194336 | tf_op jit(solution)/shard_map/all_to_all | solution.py:48
  89.6 16.8 %scatter_fusion = f32[768,512]{1,0:T(8,128)} fusion(f32[768,512]{1,0:T(8,128)} %copy.18, s32[2048]{0:T(1024)S(1)} %bitcast.74, f32[2048,512]{1,0:T(8,128)} %bitcast.10), kind=kCustom, calls=%fused_computation.3 | custom fusion | flops 1048576 | bytes 12591104 | tf_op jit(solution)/shard_map/scatter-add | solution.py:51
  106.5 4.9 %gather_fusion = f32[768,512]{1,0:T(8,128)} fusion(f32[768,512]{1,0:T(8,128)} %scatter_fusion, s32[1024]{0:T(1024)S(1)} %pad_clamp_fusion), kind=kCustom, calls=%fused_computation | custom fusion | bytes 3148800 | tf_op jit(solution)/shard_map/gather | solution.py:53
  111.4 0.0 all-gather.3.cloned.1.call-done
  111.4 0.0 copy-start.3
  111.4 9.7 %fusion.15 = f32[512,768]{1,0:T(8,128)S(1)} fusion(f32[768,512]{1,0:T(8,128)} %gather_fusion, f32[768,768]{1,0:T(8,128)} %all-gather.3.cloned.1.call-done), kind=kOutput, calls=%fused_computation.39 | convolution fusion | flops 3623878656 | bytes 5505024 | tf_op jit(solution)/shard_map/dot_general | solution.py:54
  121.1 0.0 copy-start.1
  121.1 1.1 copy-done.1
  122.3 0.0 copy-done.3
  122.3 1.4 convolution_multiply_fusion.1
  123.7 1.2 collective-permute-start
  124.8 0.0 all-gather.5.cloned.1.call-done
  124.8 0.0 copy-start.2
  124.8 2.5 %fusion.6 = f32[512,768]{1,0:T(8,128)S(1)} fusion(f32[512,128]{1,0:T(8,128)S(1)} %convolution_multiply_fusion.1, f32[2,2,768,128]{3,2,1,0:T(8,128)} %bitcast.66), kind=kOutput, calls=%fused_computation.19 | convolution fusion | flops 603979776 | bytes 2228224 | tf_op jit(solution)/shard_map/dot_general | solution.py:83
  127.3 0.0 copy-start.4
  127.3 3.6 %collective-permute-done = f32[128,512]{0,1:T(8,128)} collective-permute-done((f32[128,512]{0,1:T(8,128)S(1)}, f32[128,512]{0,1:T(8,128)}, u32[]{:S(2)}, u32[]{:S(2)}) %collective-permute-start) | collective-permute-done | bytes 262176 | tf_op jit(solution)/shard_map/ppermute | solution.py:10
  130.9 0.0 copy-done.2
  130.9 2.5 %add_subtract_fusion = f32[512,768]{1,0:T(8,128)S(1)} fusion(f32[512,768]{1,0:T(8,128)S(1)} %copy-done.2, f32[512,768]{1,0:T(8,128)S(1)} %fusion.6, f32[128,512]{0,1:T(8,128)} %collective-permute-done, f32[2,2,768,128]{3,2,1,0:T(8,128)} %bitcast.67), kind=kOutput, calls=%fused_computation.8 | convolution fusion | flops 604766208 | bytes 5373952 | tf_op jit(solution)/shard_map/dot_general | solution.py:81
  133.4 0.0 copy-done.4
  133.4 0.0 copy-start.5
  133.4 1.4 fusion.2
  134.8 1.1 collective-permute-start.1
  135.9 6.7 %collective-permute-done.1 = f32[128,512]{0,1:T(8,128)S(1)} collective-permute-done((f32[128,512]{0,1:T(8,128)S(1)}, f32[128,512]{0,1:T(8,128)S(1)}, u32[]{:S(2)}, u32[]{:S(2)}) %collective-permute-start.1) | collective-permute-done | bytes 262176 | tf_op jit(solution)/shard_map/ppermute | solution.py:10
  142.6 0.1 collective-permute-start.2
  142.7 0.0 copy-done.5
  142.7 1.4 fusion.5
  144.1 6.5 %collective-permute-done.2 = f32[128,512]{0,1:T(8,128)S(1)} collective-permute-done((f32[128,512]{0,1:T(8,128)S(1)}, f32[128,512]{0,1:T(8,128)S(1)}, u32[]{:S(2)}, u32[]{:S(2)}) %collective-permute-start.2) | collective-permute-done | bytes 262176 | tf_op jit(solution)/shard_map/ppermute | solution.py:10
  150.6 2.6 %subtract_bitcast_fusion = f32[768,512]{0,1:T(8,128)} fusion(f32[512,768]{1,0:T(8,128)S(1)} %add_subtract_fusion, f32[512,768]{1,0:T(8,128)S(1)} %fusion.5, f32[128,512]{0,1:T(8,128)S(1)} %collective-permute-done.2, f32[2,2,768,128]{3,2,1,0:T(8,128)S(1)} %bitcast.69), kind=kOutput, calls=%fused_computation.7 | convolution fusion | flops 604766208 | bytes 5373952 | tf_op jit(solution)/shard_map/dot_general | solution.py:81
  153.1 3.0 %copy.13 = f32[768,512]{1,0:T(8,128)} copy(f32[768,512]{0,1:T(8,128)} %subtract_bitcast_fusion) | data formatting | bytes 3145728 | tf_op jit(solution)/shard_map/sub | solution.py:86
  156.1 7.4 %scatter_custom_fusion.3 = f32[768,512]{1,0:T(8,128)} fusion(s32[768]{0:T(1024)S(1)} %fusion.13, f32[768,512]{1,0:T(8,128)} %copy.13, f32[]{:T(128)} %constant.7.clone.1), kind=kCustom, calls=%fused_computation.12 | custom fusion | bytes 1573376 | tf_op jit(solution)/shard_map/scatter | solution.py:87
  (9 shorter events, 0.1 us)
Async XLA Ops:
  6.5 13.8 %copy-start = (f32[1024,768]{1,0:T(8,128)S(1)}, f32[1024,768]{1,0:T(8,128)}, u32[]{:S(2)}) copy-start(f32[1024,768]{1,0:T(8,128)} %param.12) | copy-start | bytes 9437188
  6.5 2.9 %copy-start.6 = (s32[1024,1]{0,1:T(1,128)S(1)}, s32[1024,1]{0,1:T(1,128)}, u32[]{:S(2)}) copy-start(s32[1024,1]{0,1:T(1,128)} %param.13) | copy-start | bytes 12292
  6.5 4.4 %copy-start.8 = (s32[1024]{0:T(1024)S(1)}, s32[1024]{0:T(1024)}, u32[]{:S(2)}) copy-start(s32[1024]{0:T(1024)} %param.14) | copy-start | bytes 12292
  6.5 104.8 %all-gather.3.cloned.1.call-start = ((), (), s32[]{:S(2)}) async-start(), calls=%async_computation.2 | async-start | bytes 2433024 | tf_op jit(solution)/shard_map/all_gather | solution.py:55
  16.0 19.8 %all-to-all-start = ((f32[4,512,1]{1,2,0:T(1,128)}), f32[4,512,1]{1,2,0:T(1,128)S(1)}, u32[]{:S(2)}, u32[]{:S(2)}) async-start(f32[4,512,1]{1,2,0:T(1,128)} %bitcast.6), calls=%async_computation | async-start | bytes 16384 | tf_op jit(solution)/shard_map/all_to_all | solution.py:49
  35.8 5.7 %copy-start.9 = (s32[1,768]{1,0:T(1,128)S(1)}, s32[1,768]{1,0:T(1,128)}, u32[]{:S(2)}) copy-start(s32[1,768]{1,0:T(1,128)} %param.11) | copy-start | bytes 9220
  35.8 5.8 %copy-start.7 = (f32[2,24,128]{2,1,0:T(8,128)S(1)}, f32[2,24,128]{2,1,0:T(8,128)}, u32[]{:S(2)}) copy-start(f32[2,24,128]{2,1,0:T(8,128)} %param.16) | copy-start | bytes 73732
  35.8 53.9 %all-to-all-start.1 = ((f32[4,512,512]{2,1,0:T(8,128)}), f32[4,512,512]{2,1,0:T(8,128)}, u32[]{:S(2)}, u32[]{:S(2)}) async-start(f32[4,512,512]{2,1,0:T(8,128)} %bitcast.65), calls=%async_computation.1 | async-start | bytes 8388608 | tf_op jit(solution)/shard_map/all_to_all | solution.py:48
  40.8 84.1 %all-gather.5.cloned.1.call-start = ((), (), s32[]{:S(2)}) async-start(), calls=%async_computation.3 | async-start | bytes 1622016 | tf_op jit(solution)/shard_map/all_gather | solution.py:64
  111.4 10.9 %copy-start.3 = (f32[2,768,128]{2,1,0:T(8,128)S(1)}, f32[2,768,128]{2,1,0:T(8,128)}, u32[]{:S(2)}) copy-start(f32[2,768,128]{2,1,0:T(8,128)} %all_gather.10) | copy-start | bytes 2359300
  121.1 1.1 copy-start.1
  123.7 7.2 %collective-permute-start = (f32[128,512]{0,1:T(8,128)S(1)}, f32[128,512]{0,1:T(8,128)}, u32[]{:S(2)}, u32[]{:S(2)}) collective-permute-start(f32[128,512]{0,1:T(8,128)S(1)} %bitcast.70), channel_id=1, source_target_pairs={{0,32},{32,0},{64,96},{96,64},{1,33},{33,1},{65,97},{97,65},{2,34}... | collective-permute-start | bytes 786440 | tf_op jit(solution)/shard_map/ppermute | solution.py:10
  124.8 6.1 %copy-start.2 = (f32[512,768]{1,0:T(8,128)S(1)}, f32[512,768]{1,0:T(8,128)}, u32[]{:S(2)}) copy-start(f32[512,768]{1,0:T(8,128)} %copy-done.1) | copy-start | bytes 4718596
  127.3 6.1 %copy-start.4 = (f32[2,768,128]{2,1,0:T(8,128)S(1)}, f32[2,768,128]{2,1,0:T(8,128)}, u32[]{:S(2)}) copy-start(f32[2,768,128]{2,1,0:T(8,128)} %all_gather.10) | copy-start | bytes 2359300
  133.4 9.3 %copy-start.5 = (f32[4,768,128]{2,1,0:T(8,128)S(1)}, f32[4,768,128]{2,1,0:T(8,128)}, u32[]{:S(2)}) copy-start(f32[4,768,128]{2,1,0:T(8,128)} %all-gather.5.cloned.1.call-done) | copy-start | bytes 4718596
  134.8 7.8 %collective-permute-start.1 = (f32[128,512]{0,1:T(8,128)S(1)}, f32[128,512]{0,1:T(8,128)S(1)}, u32[]{:S(2)}, u32[]{:S(2)}) collective-permute-start(f32[128,512]{0,1:T(8,128)S(1)} %fusion.2), channel_id=1, source_target_pairs={{0,32},{32,0},{64,96},{96,64},{1,33},{33,1},{65,97},{97,65},{2,34}... | collective-permute-start | bytes 786440 | tf_op jit(solution)/shard_map/ppermute | solution.py:10
  142.6 8.0 %collective-permute-start.2 = (f32[128,512]{0,1:T(8,128)S(1)}, f32[128,512]{0,1:T(8,128)S(1)}, u32[]{:S(2)}, u32[]{:S(2)}) collective-permute-start(f32[128,512]{0,1:T(8,128)S(1)} %add.52), channel_id=1, source_target_pairs={{0,64},{32,96},{64,0},{96,32},{1,65},{33,97},{65,1},{97,33},{2,66}... | collective-permute-start | bytes 786440 | tf_op jit(solution)/shard_map/ppermute | solution.py:10
Sparse Core Ops, SparseCore 0:
  9.6 46.8 all-gather.2
  58.9 42.7 all-gather.4
where the time goes:
time: 171 us; the launch traced here: 170 us
  waiting for transfers between devices  36.6 us (21%)
  local copies, waits for them, and re-layouts  32 us (19%)
  matrix products  29.3 us (17%)
  blocking collectives  28.9 us (17%)
  other arithmetic  18.3 us (11%)
  between operations  13.6 us (8%)
  starting transfers between devices  11.7 us (7%)
    all_gather x1, blocking collectives, per_device(): lax.all_gather(basis_v, 'col', axis=1, tiled=True)  28.9 us
    all_to_all x1, waiting for transfers between devices, per_device(): lax.all_to_all(bucket_vals, 'leaf', split_axis=0, concat_axis=0, tiled=True)  19.2 us
    scatter-add x1, other arithmetic, per_device(): assembled = incident.at[arrived_slots.astype(jnp.int32)].add(arrived_vals)  16.8 us
    ppermute x3, waiting for transfers between devices, partner(): lax.ppermute(value, axis, [(i, i ^ 1 << distance) for i in range(lax.axis...  16.7 us
    dot_general x1, matrix products, per_device(): jnp.dot(lax.all_gather(leaf_inverse, 'col', axis=0, tiled=True), ordered,...  9.72 us
    dot_general x1, matrix products, per_device(): jnp.dot(near_quad, sources, precision=high, preferred_element_type=jnp.fl...  7.81 us
    scatter x1, local copies, waits for them, and re-layouts, per_device(): jnp.zeros((leaf_count * capacity, rhs_local), jnp.float32).at[placing]  7.6 us
    scatter x1, local copies, waits for them, and re-layouts, per_device(): jnp.zeros((leaf_rows, rhs_local), jnp.float32).at[order_row].set(state)  7.38 us
  transfers between devices with their start and end apart: 7, of which 4 were waited for; matrix products, arithmetic and copies ran while one was open for 34% of the time, Pallas kernels for 0%

commit v1 on v0

v1 whole, which is shorter than its diff:
```python
import functools
import math

import jax
import jax.numpy as jnp
from jax import lax
from jax.experimental import pallas as pl
from jax.experimental.pallas import tpu as pltpu
from jax.sharding import PartitionSpec as P

MESH = pl.DeviceIdType.MESH
F32 = jnp.float32
BF16 = jnp.bfloat16
LANES = 128
RING = 4


def halves(value):
    top = value.astype(BF16)
    return top, (value - top.astype(F32)).astype(BF16)


def dot(a, b):
    return jnp.dot(a, b, preferred_element_type=F32)


def dot3(a_hi, a_lo, b_hi, b_lo):
    return dot(a_hi, b_hi) + dot(a_hi, b_lo) + dot(a_lo, b_hi)


def tiles(count, size, body):
    def step(index, carry):
        body(pl.ds(pl.multiple_of(index * size, size), size))
        return carry

    lax.fori_loop(0, count // size, step, 0)


class Place:
    def __init__(self):
        self.leaf = lax.axis_index("leaf")
        self.col = lax.axis_index("col")
        self.core = self.col % 2
        y = (self.col // 2) % RING
        z = self.col // (2 * RING)
        self.d1 = y * (1 - self.core) + z * self.core
        self.d2 = z * (1 - self.core) + y * self.core
        self.twin = (self.leaf, self.col + 1 - 2 * self.core)
        self.mate = (self.leaf + 1 - 2 * (self.leaf % 2), self.col)
        self.cross = (3 - self.leaf, self.col)
        self.right1 = (self.leaf, self.index(self.core, 0, 1))
        self.left1 = (self.leaf, self.index(self.core, 0, RING - 1))
        self.right2 = (self.leaf, self.index(self.core, 1, 0))
        self.left2 = (self.leaf, self.index(self.core, RING - 1, 0))

    def index(self, core, off2, off1):
        a, b = (self.d2 + off2) % RING, (self.d1 + off1) % RING
        return (a * 2 * RING + b * 2) * (1 - core) + (b * 2 * RING + a * 2 + 1) * core

    def twin_index(self, off2, off1):
        core = 1 - self.core
        a, b = (self.d1 + off2) % RING, (self.d2 + off1) % RING
        return (a * 2 * RING + b * 2) * (1 - core) + (b * 2 * RING + a * 2 + 1) * core


class Gather:
    def __init__(self, place, buf, send_sem, recv_sem):
        self.p, self.buf, self.ss, self.rs = place, buf, send_sem, recv_sem
        self.half = buf.shape[2] // 2
        self.started = []

    def piece(self, off2, off1, part=None):
        ref = self.buf.at[self.p.index(self.p.core, off2, off1)]
        return ref if part is None else ref.at[:, pl.ds(part * self.half, self.half)]

    def send(self, ref, sem, device):
        copy = pltpu.make_async_remote_copy(
            src_ref=ref, dst_ref=ref, send_sem=self.ss.at[sem], recv_sem=self.rs.at[sem],
            device_id=device, device_id_type=MESH,
        )
        copy.start()
        self.started.append(copy)

    def recv(self, ref, sem):
        pltpu.make_async_remote_copy(
            src_ref=ref, dst_ref=ref, send_sem=self.ss.at[sem], recv_sem=self.rs.at[sem],
            device_id=self.p.twin, device_id_type=MESH,
        ).wait_recv()

    def ring1(self):
        self.send(self.piece(0, 0), 0, self.p.right1)
        self.send(self.piece(0, 0), 1, self.p.left1)

    def ring1_pass(self):
        self.recv(self.piece(0, 3), 0)
        self.send(self.piece(0, 3, 0), 2, self.p.right1)
        self.recv(self.piece(0, 1), 1)
        self.send(self.piece(0, 1, 1), 3, self.p.left1)

    def ring1_end(self):
        self.recv(self.piece(0, 2, 0), 2)
        self.recv(self.piece(0, 2, 1), 3)

    def ring2(self, off1):
        self.send(self.piece(0, off1), 4 + off1, self.p.right2)
        self.send(self.piece(0, off1), 8 + off1, self.p.left2)

    def ring2_pass(self, off1):
        self.recv(self.piece(3, off1), 4 + off1)
        if off1 in (0, 3):
            self.send(self.piece(3, off1), 12 + off1, self.p.right2)
        self.recv(self.piece(1, off1), 8 + off1)
        if off1 in (1, 2):
            self.send(self.piece(1, off1), 12 + off1, self.p.left2)

    def ring2_end(self, off1):
        self.recv(self.piece(2, off1), 12 + off1)

    def to_twin(self, off2, off1):
        self.send(self.piece(off2, off1), 16 + 4 * off2 + off1, self.p.twin)

    def from_twin(self):
        for off2 in range(RING):
            for off1 in range(RING):
                ref = self.buf.at[self.p.twin_index(off2, off1)]
                self.recv(ref, 16 + 4 * off2 + off1)

    def finish(self):
        for copy in self.started:
            copy.wait_send()


def kernel(
    tree, owner, slot, inverse, basis_v, basis_w, incident, sources, near_quad, out,
    nq, s_own, x, nqp, wt, key_out, key_in, s_in, y_out, y_in, z_out, z_in, t_out, t_in, m_out, m_in, acc,
    nq_hi, nq_lo, s_hi, s_lo, p_hi, p_lo, oh, gt, vt_hi, vt_lo, b_hi, b_lo, ws_hi, ws_lo, wall_hi, wall_lo,
    k_hi, k_lo, x_hi, x_lo, c_hi, c_lo,
    gsend, grecv, csend, crecv, osend, orecv, load_sem, out_sem,
):
    leaf, cols = incident.shape
    near = near_quad.shape[0]
    rank = basis_v.shape[2]
    part = near // nqp.shape[0]
    chunks = cols // LANES
    big = min(256, leaf)
    wide = min(256, cols)
    place = Place()
    mine = place.col
    started = []

    def send(src, dst, sems, index, device):
        copy = pltpu.make_async_remote_copy(
            src_ref=src, dst_ref=dst, send_sem=sems[0].at[index], recv_sem=sems[1].at[index],
            device_id=device, device_id_type=MESH,
        )
        copy.start()
        started.append(copy)
        return copy

    def left(copy):
        copy.wait_send()
        started[:] = [other for other in started if other is not copy]

    def lane(i):
        return pl.ds(i * LANES, LANES)

    loads = [
        pltpu.make_async_copy(src, dst, load_sem.at[i])
        for i, (src, dst) in enumerate(((near_quad, nq), (sources, s_own), (incident, x)))
    ]
    for copy in loads:
        copy.start()
    key_out[...] = jnp.broadcast_to(owner[...] * leaf + slot[...], key_out.shape)

    barrier = pltpu.get_barrier_semaphore()
    neighbours = (
        place.mate, place.cross, place.twin, place.right1, place.left1, place.right2, place.left2
    )
    for device in neighbours:
        pl.semaphore_signal(barrier, inc=1, device_id=device, device_id_type=MESH)
    pl.semaphore_wait(barrier, len(neighbours))

    once, per = (osend, orecv), (csend, crecv)
    rows_mine = pl.ds(pl.multiple_of(mine * part, part), part)
    near_swap = send(near_quad.at[rows_mine], nqp.at[mine], once, 0, place.mate)
    key_swap = send(key_out, key_in, once, 1, place.mate)
    source_swaps = []

    def swap_sources(i):
        source_swaps.append(send(sources.at[:, lane(i)], s_in.at[i], per, (0, i), place.mate))

    for i in range(min(2, chunks)):
        swap_sources(i)

    near_g = Gather(place, nqp, gsend.at[0], grecv.at[0])
    wt_g = Gather(place, wt, gsend.at[1], grecv.at[1])

    def make_gt(rows):
        number = rows.start + lax.broadcasted_iota(jnp.int32, (rows.size, leaf), 0)
        gt[rows, :] = jnp.where(number == tree[...], 1.0, 0.0).astype(BF16)

    tiles(leaf, LANES, make_gt)
    nt = (((1,), (1,)), ((), ()))
    top, low = halves(inverse[...])
    wt[mine, :, pl.ds(0, leaf)] = lax.dot_general(
        top, gt[...], nt, preferred_element_type=F32
    ) + lax.dot_general(low, gt[...], nt, preferred_element_type=F32)
    for k in range(4):
        wt[mine, :, pl.ds(leaf + k * rank, rank)] = basis_w[k // 2, k % 2]
    for k in range(2):
        wt[mine, :, pl.ds(leaf + (4 + k) * rank, rank)] = basis_v[k]
    wt_g.ring1()
    wt_g.ring2(0)

    def make_one_hot(which, key, device):
        base = device[0] * leaf

        def body(rows):
            number = base + rows.start + lax.broadcasted_iota(jnp.int32, (rows.size, near), 0)
            oh[which, rows, :] = jnp.where(number == key[0:1, :], 1.0, 0.0).astype(BF16)

        tiles(leaf, LANES, body)

    me = (place.leaf, place.col)
    make_one_hot(0, key_out, me)
    make_one_hot(1, key_out, place.cross)
    loads[0].wait()

    def split_own(rows):
        nq_hi[rows, :], nq_lo[rows, :] = halves(nq[rows, :])

    tiles(near, LANES, split_own)

    near_swap.wait_recv()
    near_g.ring1()
    near_g.ring2(0)
    near_g.to_twin(0, 0)

    loads[1].wait()

    def split_sources(rows):
        s_hi[rows, :], s_lo[rows, :] = halves(s_own[rows, :])

    tiles(leaf, LANES, split_sources)

    def own_partial(block):
        def body(rows):
            r = dot3(nq_hi[rows, :], nq_lo[rows, :], s_hi[:, block], s_lo[:, block])
            p_hi[rows, block], p_lo[rows, block] = halves(r)

        tiles(near, big, body)

    blocks = [pl.ds(k * wide, wide) for k in range(cols // wide)]
    for block in blocks[: len(blocks) // 2]:
        own_partial(block)
    near_g.ring1_pass()
    for off1 in (3, 1):
        near_g.ring2(off1)
        near_g.to_twin(0, off1)
    for block in blocks[len(blocks) // 2 :]:
        own_partial(block)
    near_g.ring1_end()
    near_g.ring2(2)
    near_g.to_twin(0, 2)
    wt_g.ring1_pass()

    loads[2].wait()

    def own_sums(block):
        def body(rows):
            x[rows, block] += dot(oh[0, rows, :], p_hi[:, block]) + dot(oh[0, rows, :], p_lo[:, block])
            r = dot(oh[1, rows, :], p_hi[:, block]) + dot(oh[1, rows, :], p_lo[:, block])
            for k in range(wide // LANES):
                y_out[block.start // LANES + k, rows, :] = r[:, k * LANES : (k + 1) * LANES]

        tiles(leaf, big, body)

    for block in blocks[: len(blocks) // 2]:
        own_sums(block)
    wt_g.ring1_end()
    wt_g.to_twin(0, 0)
    wt_g.to_twin(0, 1)
    wt_g.to_twin(0, 2)
    wt_g.to_twin(0, 3)
    for off1 in (0, 3, 1):
        near_g.ring2_pass(off1)
        near_g.to_twin(3, off1)
        near_g.to_twin(1, off1)
    for block in blocks[len(blocks) // 2 :]:
        own_sums(block)
    near_g.ring2_pass(2)
    near_g.to_twin(3, 2)
    near_g.to_twin(1, 2)
    for off1 in (3, 1, 2):
        wt_g.ring2(off1)
    if chunks > 2:
        left(source_swaps[0])
        swap_sources(2)
    key_swap.wait_recv()
    make_one_hot(2, key_in, me)
    make_one_hot(3, key_in, place.cross)
    for off1 in (0, 3, 1, 2):
        near_g.ring2_end(off1)
        near_g.to_twin(2, off1)
    near_g.from_twin()

    def split_partner(index, carry):
        rows = pl.ds(pl.multiple_of(index * part, part), part)
        nq_hi[rows, :], nq_lo[rows, :] = halves(nqp[index])
        return carry

    lax.fori_loop(0, nqp.shape[0], split_partner, 0)

    sum_swaps, z_swaps, t_swaps, stores = {}, {}, {}, {}

    def near_chunk(i):
        source_swaps[i].wait_recv()

        def split(rows):
            s_hi[rows, lane(i)], s_lo[rows, lane(i)] = halves(s_in[i, rows, :])

        tiles(leaf, LANES, split)

        def partial(rows):
            r = dot3(nq_hi[rows, :], nq_lo[rows, :], s_hi[:, lane(i)], s_lo[:, lane(i)])
            p_hi[rows, lane(i)], p_lo[rows, lane(i)] = halves(r)

        tiles(near, big, partial)

        def across(rows):
            y_out[i, rows, :] += dot(oh[3, rows, :], p_hi[:, lane(i)]) + dot(
                oh[3, rows, :], p_lo[:, lane(i)]
            )

        tiles(leaf, big, across)
        sum_swaps[i] = send(y_out.at[i], y_in.at[i], per, (1, i), place.cross)

        def here(rows):
            x[rows, lane(i)] += dot(oh[2, rows, :], p_hi[:, lane(i)]) + dot(
                oh[2, rows, :], p_lo[:, lane(i)]
            )

        tiles(leaf, big, here)

    def weights():
        def split(index, carry):
            count = 2 * inverse.shape[0]
            rows = pl.ds(pl.multiple_of(index * count, 16), count)
            both = wt[pl.ds(2 * index, 2), :, pl.ds(0, leaf + 4 * rank)]
            ws_hi[rows, :], ws_lo[rows, :] = halves(both.reshape(count, leaf + 4 * rank))
            return carry

        lax.fori_loop(0, wt.shape[0] // 2, split, 0)
        for k in range(2):
            v = wt[:, :, pl.ds(leaf + (4 + k) * rank, rank)].reshape(leaf, rank)
            v = v * (1.0 / math.sqrt(2**k * leaf))
            rows = pl.ds(k * rank, rank)
            vt_hi[rows, :], vt_lo[rows, :] = halves(v.T)
        last = pl.ds(rank, rank)
        first_w = pl.ds(leaf, 2 * rank)
        m_out[...] = dot3(vt_hi[last, :], vt_lo[last, :], ws_hi[:, first_w], ws_lo[:, first_w])
        swap = send(m_out, m_in, once, 2, place.mate)
        step = min(256, leaf)
        for k in range(leaf // step):
            block = pl.ds(k * step, step)

            def body(rows):
                r = dot3(vt_hi[rows, :], vt_lo[rows, :], ws_hi[:, block], ws_lo[:, block])
                b_hi[rows, block], b_lo[rows, block] = halves(r)

            tiles(2 * rank, rank, body)
        for k in range((leaf + 4 * rank) // step):
            block = pl.ds(k * step, step)
            sign = 1.0 if k * step < leaf else -1.0

            def body(rows):
                wall_hi[rows, block] = (dot(gt[rows, :], ws_hi[:, block]) * sign).astype(BF16)
                wall_lo[rows, block] = (dot(gt[rows, :], ws_lo[:, block]) * sign).astype(BF16)

            tiles(leaf, big, body)
        swap.wait_recv()
        one, two = pl.ds(0, rank), pl.ds(rank, rank)
        k_hi[:, one], k_lo[:, one] = halves(m_out[:, one] + m_in[:, two])
        k_hi[:, two], k_lo[:, two] = halves(m_out[:, two] + m_in[:, one])

    def apply(rows, at, size, v_hi, v_lo):
        block = pl.ds(at, size)
        return dot3(wall_hi[rows, block], wall_lo[rows, block], v_hi, v_lo)

    def first(i):
        sum_swaps[i].wait_recv()

        def split(rows):
            x_hi[rows, :], x_lo[rows, :] = halves(x[rows, lane(i)] + y_in[i, rows, :])

        tiles(leaf, LANES, split)

        def coefficients(rows):
            z_out[i, rows, :] = dot3(b_hi[rows, :], b_lo[rows, :], x_hi[...], x_lo[...])

        tiles(2 * rank, rank, coefficients)
        z_swaps[i] = send(z_out.at[i], z_in.at[i], per, (2, i), place.mate)

        def state(rows):
            acc[rows, lane(i)] = apply(rows, 0, leaf, x_hi[...], x_lo[...])

        tiles(leaf, big, state)

    def second(i):
        z_swaps[i].wait_recv()
        one, two = pl.ds(0, rank), pl.ds(rank, rank)
        c_hi[one, :], c_lo[one, :] = halves(z_in[i, one, :])
        c_hi[two, :], c_lo[two, :] = halves(z_out[i, one, :])
        change = dot3(k_hi[...], k_lo[...], c_hi[...], c_lo[...])
        total = z_out[i, two, :] + z_in[i, two, :] - change
        t_out[i] = total
        t_swaps[i] = send(t_out.at[i], t_in.at[i], per, (3, i), place.cross)
        t_hi, t_lo = halves(total)

        def update(rows):
            acc[rows, lane(i)] += apply(rows, leaf, 2 * rank, c_hi[...], c_lo[...]) + apply(
                rows, leaf + 3 * rank, rank, t_hi, t_lo
            )

        tiles(leaf, big, update)

    def third(i):
        t_swaps[i].wait_recv()
        t_hi, t_lo = halves(t_in[i])

        def update(rows):
            acc[rows, lane(i)] += apply(rows, leaf + 2 * rank, rank, t_hi, t_lo)

        tiles(leaf, big, update)
        stores[i] = pltpu.make_async_copy(acc.at[:, lane(i)], out.at[:, lane(i)], out_sem.at[i])
        stores[i].start()

    near_chunk(0)
    for off1 in (0, 3, 1, 2):
        wt_g.ring2_pass(off1)
        wt_g.to_twin(3, off1)
        wt_g.to_twin(1, off1)
    if chunks > 3:
        left(source_swaps[1])
        swap_sources(3)
    near_chunk(1)
    for off1 in (0, 3, 1, 2):
        wt_g.ring2_end(off1)
        wt_g.to_twin(2, off1)
    for i in range(2, chunks - 1):
        near_chunk(i)
    wt_g.from_twin()
    weights()
    first(0)
    if chunks > 2:
        near_chunk(chunks - 1)
    for i in range(1, chunks):
        first(i)
        second(i - 1)
        if i > 1:
            third(i - 2)
    second(chunks - 1)
    if chunks > 1:
        third(chunks - 2)
    third(chunks - 1)

    for i in range(chunks):
        stores[i].wait()
    for copy in started:
        copy.wait_send()
    near_g.finish()
    wt_g.finish()


def per_device(
    incident, sources, tree_order, near_quad, near_owner, near_slot, leaf_inverse, basis_v, basis_w
):
    leaf, cols = incident.shape
    near = near_quad.shape[0]
    rank = basis_v.shape[2]
    group = lax.axis_size("col")
    rows = leaf // group
    chunks = cols // LANES
    width = leaf + 6 * rank
    vmem, sem = pltpu.VMEM, pltpu.SemaphoreType.DMA

    def f32(*shape):
        return vmem(shape, F32)

    def pair(*shape):
        return [vmem(shape, BF16), vmem(shape, BF16)]

    scratch = [
        f32(near, leaf), f32(leaf, cols), f32(leaf, cols),
        f32(group, near // group, leaf), f32(group, rows, width),
        vmem((8, near), jnp.int32), vmem((8, near), jnp.int32),
        f32(chunks, leaf, LANES), f32(chunks, leaf, LANES), f32(chunks, leaf, LANES),
        f32(chunks, 2 * rank, LANES), f32(chunks, 2 * rank, LANES),
        f32(chunks, rank, LANES), f32(chunks, rank, LANES),
        f32(rank, 2 * rank), f32(rank, 2 * rank), f32(leaf, cols),
        *pair(near, leaf), *pair(leaf, cols), *pair(near, cols),
        vmem((4, leaf, near), BF16), vmem((leaf, leaf), BF16),
        *pair(2 * rank, leaf), *pair(2 * rank, leaf),
        *pair(leaf, leaf + 4 * rank), *pair(leaf, leaf + 4 * rank),
        *pair(rank, 2 * rank), *pair(leaf, LANES), *pair(2 * rank, LANES),
        sem((2, 32)), sem((2, 32)), sem((4, chunks)), sem((4, chunks)), sem((3,)), sem((3,)),
        sem((3,)), sem((chunks,)),
    ]
    in_vmem = pl.BlockSpec(memory_space=pltpu.VMEM)
    in_any = pl.BlockSpec(memory_space=pl.ANY)
    return pl.pallas_call(
        kernel,
        out_shape=jax.ShapeDtypeStruct((leaf, cols), F32),
        in_specs=[in_vmem] * 6 + [in_any] * 3,
        out_specs=in_any,
        scratch_shapes=scratch,
        compiler_params=pltpu.CompilerParams(
            collective_id=0, has_side_effects=True, vmem_limit_bytes=60 * 1024 * 1024
        ),
        cost_estimate=pl.CostEstimate(flops=15 * 10**9, bytes_accessed=12 * 10**6, transcendentals=0),
    )(
        tree_order, near_owner.reshape(1, near), near_slot.reshape(1, near),
        leaf_inverse, basis_v, basis_w, incident, sources, near_quad,
    )


def solution(mesh):
    placed = (
        P("leaf", "col"),
        P("leaf", "col"),
        P("leaf", None),
        P("leaf", None),
        P("leaf", None),
        P("leaf"),
        P(("leaf", "col"), None),
        P(None, ("leaf", "col"), None),
        P(None, None, ("leaf", "col"), None),
    )
    return jax.shard_map(
        per_device, mesh=mesh, in_specs=placed, out_specs=P("leaf", "col"), check_vma=False
    )
```

time: 171 us -> 88.1 us (0.52)
  Pallas kernels: 0 us -> 85.2 us
  waiting for transfers between devices: 36.6 us -> 0 us
  local copies, waits for them, and re-layouts: 32 us -> 2.67 us
  matrix products: 29.3 us -> 0 us
  blocking collectives: 28.9 us -> 0 us
  other arithmetic: 18.3 us -> 0 us
  between operations: 13.6 us -> 0.01 us
  starting transfers between devices: 11.7 us -> 0 us
    pallas_call x0 -> x1, Pallas kernels: none -> 85.2 us  [per_device(): pl.pallas_call(kernel, out_shape=jax.ShapeDtypeStruct((leaf, cols), F32),...]
    dot_general x8 -> x0, matrix products: 29.3 us -> none  [the longest x1 9.72 us: per_device(): jnp.dot(lax.all_gather(leaf_inverse, 'col', axis=0, tiled=True), ordered,...]
    all_gather x1 -> x0, blocking collectives: 28.9 us -> none  [per_device(): lax.all_gather(basis_v, 'col', axis=1, tiled=True)]
    scatter x3 -> x0, local copies, waits for them, and re-layouts: 19.9 us -> none  [the longest x1 7.6 us: per_device(): jnp.zeros((leaf_count * capacity, rhs_local), jnp.float32).at[placing]]
    all_to_all x2 -> x0, waiting for transfers between devices: 19.2 us -> none  [the longest x1 19.2 us: per_device(): lax.all_to_all(bucket_vals, 'leaf', split_axis=0, concat_axis=0, tiled=True)]
    scatter-add x1 -> x0, other arithmetic: 16.8 us -> none  [per_device(): assembled = incident.at[arrived_slots.astype(jnp.int32)].add(arrived_vals)]
    ppermute x3 -> x0, waiting for transfers between devices: 16.7 us -> none  [partner(): lax.ppermute(value, axis, [(i, i ^ 1 << distance) for i in range(lax.axis...]
    all_to_all x2 -> x0, starting transfers between devices: 9.35 us -> none  [the longest x1 4.98 us: per_device(): lax.all_to_all(bucket_vals, 'leaf', split_axis=0, concat_axis=0, tiled=True)]
  transfers between devices with their start and end apart: 7 -> 0, of which waited for: 4 -> 0; matrix products, arithmetic and copies ran while one was open for 34% -> 0% of each run, Pallas kernels for 0% -> 0%
where the time goes in v1:
time: 88.1 us; the launch traced here: 87.9 us
  Pallas kernels  85.2 us (97%)
  local copies, waits for them, and re-layouts  2.67 us (3%)
    pallas_call x1, Pallas kernels, per_device(): pl.pallas_call(kernel, out_shape=jax.ShapeDtypeStruct((leaf, cols), F32),...  85.2 us
    unnamed x1, local copies, waits for them, and re-layouts  2.67 us

profile of v1, /device:TPU:0, one launch (start us, length us, event | category | flops | bytes accessed | tf_op | source)
XLA Modules:
  0.0 87.9 jit_solution(6983563025260636361)
XLA Ops:
  0.0 85.2 %shard_map.91 = f32[768,512]{1,0:T(8,128)} custom-call(s32[1,768]{1,0:T(1,128)} %tree.1, s32[1,1024]{1,0:T(1,128)} %bitcast.2, s32[1,1024]{1,0:T(1,128)} %bitcast.3, f32[24,768]{1,0:T(8,128)} %inverse.1, f32[2,24,128]{2,1,0:T(8,128)} %basis_v.1, f32[2,2,24,128]{3,2,1,0:T(8,128)} %basis_w.1, f32[768,512]{1,0:T(8,128)} %incident.1, f32[768,512]{1,0:T(8,128)} %sources.1, ...), custom_call_target="tpu_custom_call" | custom-call | flops 15000000512 | bytes 12000000 | tf_op jit(solution)/shard_map/pallas_call | solution.py:511
  85.2 2.7 %copy.11 = f32[768,512]{1,0:T(8,128)} copy(f32[768,512]{1,0:T(8,128)} %shard_map.91) | data formatting | bytes 3145728

commit v2 on v1

v2 whole, which is shorter than its diff:
```python
import functools
import math

import jax
import jax.numpy as jnp
from jax import lax
from jax.experimental import pallas as pl
from jax.experimental.pallas import tpu as pltpu
from jax.sharding import PartitionSpec as P

MESH = pl.DeviceIdType.MESH
F32 = jnp.float32
BF16 = jnp.bfloat16
LANES = 128
RING = 4


def halves(value):
    top = value.astype(BF16)
    return top, (value - top.astype(F32)).astype(BF16)


def dot(a, b):
    return jnp.dot(a, b, preferred_element_type=F32)


def dot3(a_hi, a_lo, b_hi, b_lo):
    return dot(a_hi, b_hi) + dot(a_hi, b_lo) + dot(a_lo, b_hi)


def beside(value):
    return jnp.concatenate(halves(value), axis=1)


def fold(wide):
    return wide[:, :LANES] + wide[:, LANES:]


def dot_beside(a_hi, a_lo, b):
    return fold(dot(a_hi, b)) + dot(a_lo, b[:, :LANES])


def tiles(count, size, body):
    def step(index, carry):
        body(pl.ds(pl.multiple_of(index * size, size), size))
        return carry

    lax.fori_loop(0, count // size, step, 0)


class Place:
    def __init__(self):
        self.leaf = lax.axis_index("leaf")
        self.col = lax.axis_index("col")
        self.core = self.col % 2
        y = (self.col // 2) % RING
        z = self.col // (2 * RING)
        self.d1 = y * (1 - self.core) + z * self.core
        self.d2 = z * (1 - self.core) + y * self.core
        self.twin = (self.leaf, self.col + 1 - 2 * self.core)
        self.mate = (self.leaf + 1 - 2 * (self.leaf % 2), self.col)
        self.cross = (3 - self.leaf, self.col)
        self.right1 = (self.leaf, self.index(self.core, 0, 1))
        self.left1 = (self.leaf, self.index(self.core, 0, RING - 1))
        self.opposite1 = (self.leaf, self.index(self.core, 0, 2))
        self.far = self.leaf + 2 - 4 * (self.leaf // 2)
        self.right2 = (self.leaf, self.index(self.core, 1, 0))
        self.left2 = (self.leaf, self.index(self.core, RING - 1, 0))

    def index(self, core, off2, off1):
        a, b = (self.d2 + off2) % RING, (self.d1 + off1) % RING
        return (a * 2 * RING + b * 2) * (1 - core) + (b * 2 * RING + a * 2 + 1) * core

    def twin_index(self, off2, off1):
        core = 1 - self.core
        a, b = (self.d1 + off2) % RING, (self.d2 + off1) % RING
        return (a * 2 * RING + b * 2) * (1 - core) + (b * 2 * RING + a * 2 + 1) * core


class Gather:
    def __init__(self, place, buf, send_sem, recv_sem):
        self.p, self.buf, self.ss, self.rs = place, buf, send_sem, recv_sem
        self.started = []

    def piece(self, off2, off1):
        return self.buf.at[self.p.index(self.p.core, off2, off1)]

    def send(self, ref, sem, device):
        copy = pltpu.make_async_remote_copy(
            src_ref=ref, dst_ref=ref, send_sem=self.ss.at[sem], recv_sem=self.rs.at[sem],
            device_id=device, device_id_type=MESH,
        )
        copy.start()
        self.started.append(copy)

    def recv(self, ref, sem):
        pltpu.make_async_remote_copy(
            src_ref=ref, dst_ref=ref, send_sem=self.ss.at[sem], recv_sem=self.rs.at[sem],
            device_id=self.p.twin, device_id_type=MESH,
        ).wait_recv()

    def ring1(self):
        own = self.piece(0, 0)
        self.send(own, 0, self.p.right1)
        self.send(own, 1, self.p.left1)
        self.send(own, 2, self.p.opposite1)

    def ring1_end(self):
        for sem, off1 in enumerate((3, 1, 2)):
            self.recv(self.piece(0, off1), sem)

    def ring2(self, off1):
        self.send(self.piece(0, off1), 4 + off1, self.p.right2)
        self.send(self.piece(0, off1), 8 + off1, self.p.left2)

    def ring2_pass(self, off1):
        self.recv(self.piece(3, off1), 4 + off1)
        if off1 in (0, 3):
            self.send(self.piece(3, off1), 12 + off1, self.p.right2)
        self.recv(self.piece(1, off1), 8 + off1)
        if off1 in (1, 2):
            self.send(self.piece(1, off1), 12 + off1, self.p.left2)

    def ring2_end(self, off1):
        self.recv(self.piece(2, off1), 12 + off1)

    def to_twin(self, off2, off1):
        self.send(self.piece(off2, off1), 16 + 4 * off2 + off1, self.p.twin)

    def from_twin(self):
        for off2 in range(RING):
            for off1 in range(RING):
                ref = self.buf.at[self.p.twin_index(off2, off1)]
                self.recv(ref, 16 + 4 * off2 + off1)

    def finish(self):
        for copy in self.started:
            copy.wait_send()


def kernel(
    tree_any, owner_any, slot_any, inverse_any, basis_v_any, basis_w_any, incident, sources, near_quad, out,
    tree, owner, slot, inverse, basis_v, basis_w,
    nq, s_own, x, nqp, wt, key_out, key_in, s_in, y_out, y_in, z_out, z_in, t_out, t_in, u_out, u_in, w_out, w_in,
    m_out, m_in, acc,
    nq_hi, nq_lo, s_hl, p_hl, oh, gt, vt_hi, vt_lo, b_hi, b_lo, ws_hi, ws_lo, wall_hi, wall_lo,
    k_hi, k_lo, x_hl, c_hl,
    gsend, grecv, csend, crecv, osend, orecv, load_sem, out_sem,
):
    leaf, cols = incident.shape
    near = near_quad.shape[0]
    rank = basis_v.shape[2]
    part = near // nqp.shape[0]
    chunks = cols // LANES
    last = chunks - 1
    near_tile, leaf_tile = near // 2, leaf // 2
    place = Place()
    mine = place.col
    started = []

    def lane(i):
        return pl.ds(i * LANES, LANES)

    pairs = (
        (tree_any, tree), (owner_any, owner), (slot_any, slot), (inverse_any, inverse), (basis_v_any, basis_v),
        (basis_w_any, basis_w), (near_quad, nq), (sources, s_own), (incident, x),
    )
    loads = [pltpu.make_async_copy(src, dst, load_sem.at[i]) for i, (src, dst) in enumerate(pairs)]
    barrier = pltpu.get_barrier_semaphore()
    neighbours = (
        place.mate, place.cross, place.twin, place.right1, place.left1, place.opposite1, place.right2, place.left2
    )
    for device in neighbours:
        pl.semaphore_signal(barrier, inc=1, device_id=device, device_id_type=MESH)
    for copy in loads:
        copy.start()

    def send(src, dst, sems, index, device):
        copy = pltpu.make_async_remote_copy(
            src_ref=src, dst_ref=dst, send_sem=sems[0].at[index], recv_sem=sems[1].at[index],
            device_id=device, device_id_type=MESH,
        )
        copy.start()
        started.append(copy)
        return copy

    near_g = Gather(place, nqp, gsend.at[0], grecv.at[0])
    wt_g = Gather(place, wt, gsend.at[1], grecv.at[1])

    def make_gt(rows):
        number = rows.start + lax.broadcasted_iota(jnp.int32, (rows.size, leaf), 0)
        gt[rows, :] = jnp.where(number == tree[...], 1.0, 0.0).astype(BF16)

    def make_one_hot(which, key, block):
        base = block * leaf

        def body(rows):
            number = base + rows.start + lax.broadcasted_iota(jnp.int32, (rows.size, near), 0)
            oh[which, rows, :] = jnp.where(number == key[0:1, :], 1.0, 0.0).astype(BF16)

        tiles(leaf, LANES, body)

    def split_near(rows):
        nq_hi[rows, :], nq_lo[rows, :] = halves(nq[rows, :])

    def partial(i):
        def body(rows):
            p_hl[i, rows, :] = beside(dot_beside(nq_hi[rows, :], nq_lo[rows, :], s_hl[i]))

        tiles(near, near_tile, body)

    def own_partial(i):
        def body(rows):
            s_hl[i, rows, :] = beside(s_own[rows, lane(i)])

        tiles(leaf, LANES, body)
        partial(i)

    def sums(which, i, rows):
        return fold(dot(oh[which, rows, :], p_hl[i]))

    for copy in loads[:6]:
        copy.wait()
    key_out[...] = jnp.broadcast_to(owner[...] * leaf + slot[...], key_out.shape)
    tiles(leaf, LANES, make_gt)
    nt = (((1,), (1,)), ((), ()))
    top, low = halves(inverse[...])
    wt[mine, :, pl.ds(0, leaf)] = lax.dot_general(
        top, gt[...], nt, preferred_element_type=F32
    ) + lax.dot_general(low, gt[...], nt, preferred_element_type=F32)
    for k in range(4):
        wt[mine, :, pl.ds(leaf + k * rank, rank)] = basis_w[k // 2, k % 2]
    for k in range(2):
        wt[mine, :, pl.ds(leaf + (4 + k) * rank, rank)] = basis_v[k]
    make_one_hot(1, key_out, place.cross[0])
    make_one_hot(3, key_out, place.far)
    loads[6].wait()
    tiles(near, LANES, split_near)
    loads[7].wait()
    own_partial(last)

    pl.semaphore_wait(barrier, len(neighbours))

    once, per = (osend, orecv), (csend, crecv)
    rows_mine = pl.ds(pl.multiple_of(mine * part, part), part)
    near_swap = send(near_quad.at[rows_mine], nqp.at[mine], once, 0, place.mate)
    key_swap = send(key_out, key_in, once, 1, place.mate)
    wt_g.ring1()
    wt_g.ring2(0)
    wt_g.to_twin(0, 0)
    source_swaps = [
        send(sources.at[:, lane(i)], s_in.at[i], per, (0, i), place.mate) for i in range(last)
    ]

    def last_across(rows):
        y_out[last, rows, :] = sums(1, last, rows)

    tiles(leaf, leaf_tile, last_across)
    sum_swaps = {last: send(y_out.at[last], y_in.at[last], per, (1, last), place.cross)}

    def last_far(rows):
        w_out[rows, :] = sums(3, last, rows)

    tiles(leaf, leaf_tile, last_far)
    far_swap = send(w_out, w_in, once, 3, place.cross)
    make_one_hot(2, key_out, place.mate[0])
    make_one_hot(0, key_out, place.leaf)

    near_swap.wait_recv()
    near_g.ring1()
    near_g.ring2(0)
    near_g.to_twin(0, 0)

    for i in range(last):
        own_partial(i)
    near_g.ring1_end()
    for off1 in (3, 1, 2):
        near_g.ring2(off1)
    for off1 in (3, 1, 2):
        near_g.to_twin(0, off1)
    wt_g.ring1_end()
    for off1 in (3, 1, 2):
        wt_g.to_twin(0, off1)
    loads[8].wait()

    def own_sums(i):
        def body(rows):
            x[rows, lane(i)] += sums(0, i, rows)
            if i < last:
                y_out[i, rows, :] = sums(1, i, rows)
            else:
                u_out[rows, :] = sums(2, i, rows)

        tiles(leaf, leaf_tile, body)

    own_sums(last)
    for i in range(last // 2):
        own_sums(i)
    for off1 in (0, 3, 1, 2):
        near_g.ring2_pass(off1)
    for off1 in (3, 1, 2):
        wt_g.ring2(off1)
    for off1 in (0, 3, 1, 2):
        near_g.to_twin(3, off1)
        near_g.to_twin(1, off1)
    for i in range(last // 2, last):
        own_sums(i)
    key_swap.wait_recv()
    make_one_hot(4, key_in, place.leaf)
    make_one_hot(5, key_in, place.cross[0])
    for off1 in (0, 3, 1, 2):
        near_g.ring2_end(off1)
        near_g.to_twin(2, off1)
    near_g.from_twin()

    def split_partner(index, carry):
        rows = pl.ds(pl.multiple_of(index * 2 * part, 2 * part), 2 * part)
        nq_hi[rows, :], nq_lo[rows, :] = halves(nqp[pl.ds(2 * index, 2)].reshape(2 * part, leaf))
        return carry

    lax.fori_loop(0, nqp.shape[0] // 2, split_partner, 0)

    z_swaps, t_swaps, stores = {}, {}, {}

    def near_chunk(i):
        source_swaps[i].wait_recv()

        def split(rows):
            s_hl[i, rows, :] = beside(s_in[i, rows, :])

        tiles(leaf, LANES, split)
        partial(i)

        def across(rows):
            y_out[i, rows, :] += sums(5, i, rows)

        tiles(leaf, leaf_tile, across)
        sum_swaps[i] = send(y_out.at[i], y_in.at[i], per, (1, i), place.cross)

        def here(rows):
            x[rows, lane(i)] += sums(4, i, rows)

        tiles(leaf, leaf_tile, here)

    def pass_on():
        far_swap.wait_recv()

        def body(rows):
            u_out[rows, :] += w_in[rows, :]

        tiles(leaf, LANES, body)
        return send(u_out, u_in, once, 4, place.mate)

    def weights():
        def split(index, carry):
            count = 2 * inverse.shape[0]
            rows = pl.ds(pl.multiple_of(index * count, 16), count)
            both = wt[pl.ds(2 * index, 2), :, pl.ds(0, leaf + 4 * rank)]
            ws_hi[rows, :], ws_lo[rows, :] = halves(both.reshape(count, leaf + 4 * rank))
            return carry

        lax.fori_loop(0, wt.shape[0] // 2, split, 0)
        for k in range(2):
            v = wt[:, :, pl.ds(leaf + (4 + k) * rank, rank)].reshape(leaf, rank)
            v = v * (1.0 / math.sqrt(2**k * leaf))
            rows = pl.ds(k * rank, rank)
            vt_hi[rows, :], vt_lo[rows, :] = halves(v.T)
        second_v = pl.ds(rank, rank)
        first_w = pl.ds(leaf, 2 * rank)
        m_out[...] = dot3(vt_hi[second_v, :], vt_lo[second_v, :], ws_hi[:, first_w], ws_lo[:, first_w])
        swap = send(m_out, m_in, once, 2, place.mate)
        step = min(256, leaf)
        for k in range(leaf // step):
            block = pl.ds(k * step, step)
            r = dot3(vt_hi[...], vt_lo[...], ws_hi[:, block], ws_lo[:, block])
            b_hi[:, block], b_lo[:, block] = halves(r)
        for k in range((leaf + 4 * rank) // step):
            block = pl.ds(k * step, step)
            sign = 1.0 if k * step < leaf else -1.0

            def body(rows):
                wall_hi[rows, block] = (dot(gt[rows, :], ws_hi[:, block]) * sign).astype(BF16)
                wall_lo[rows, block] = (dot(gt[rows, :], ws_lo[:, block]) * sign).astype(BF16)

            tiles(leaf, leaf_tile, body)
        return swap

    def corrections(swap):
        swap.wait_recv()
        one, two = pl.ds(0, rank), pl.ds(rank, rank)
        k_hi[:, one], k_lo[:, one] = halves(m_out[:, one] + m_in[:, two])
        k_hi[:, two], k_lo[:, two] = halves(m_out[:, two] + m_in[:, one])

    def apply(rows, at, size, value):
        block = pl.ds(at, size)
        return dot_beside(wall_hi[rows, block], wall_lo[rows, block], value)

    def first(i, more=None):
        sum_swaps[i].wait_recv()
        if more is not None:
            more.wait_recv()

        def split(rows):
            whole = x[rows, lane(i)] + y_in[i, rows, :]
            x_hl[rows, :] = beside(whole if more is None else whole + u_in[rows, :])

        tiles(leaf, LANES, split)
        z_out[i] = dot_beside(b_hi[...], b_lo[...], x_hl[...])
        z_swaps[i] = send(z_out.at[i], z_in.at[i], per, (2, i), place.mate)

        def state(rows):
            acc[rows, lane(i)] = apply(rows, 0, leaf, x_hl[...])

        tiles(leaf, leaf_tile, state)

    def second(i):
        z_swaps[i].wait_recv()
        one, two = pl.ds(0, rank), pl.ds(rank, rank)
        c_hl[one, :] = beside(z_in[i, one, :])
        c_hl[two, :] = beside(z_out[i, one, :])
        total = z_out[i, two, :] + z_in[i, two, :] - dot_beside(k_hi[...], k_lo[...], c_hl[...])
        t_out[i] = total
        t_swaps[i] = send(t_out.at[i], t_in.at[i], per, (3, i), place.cross)
        t_hl = beside(total)

        def update(rows):
            acc[rows, lane(i)] += apply(rows, leaf, 2 * rank, c_hl[...]) + apply(
                rows, leaf + 3 * rank, rank, t_hl
            )

        tiles(leaf, leaf_tile, update)

    def third(i):
        t_swaps[i].wait_recv()
        t_hl = beside(t_in[i])

        def update(rows):
            acc[rows, lane(i)] += apply(rows, leaf + 2 * rank, rank, t_hl)

        tiles(leaf, leaf_tile, update)
        stores[i] = pltpu.make_async_copy(acc.at[:, lane(i)], out.at[:, lane(i)], out_sem.at[i])
        stores[i].start()

    near_chunk(0)
    for off1 in (0, 3, 1, 2):
        wt_g.ring2_pass(off1)
        wt_g.to_twin(3, off1)
        wt_g.to_twin(1, off1)
    near_chunk(1)
    mate_sums = pass_on()
    for off1 in (0, 3, 1, 2):
        wt_g.ring2_end(off1)
        wt_g.to_twin(2, off1)
    for i in range(2, last):
        near_chunk(i)
    wt_g.from_twin()
    m_swap = weights()
    first(0)
    corrections(m_swap)
    first(last, mate_sums)
    second(0)
    first(1)
    second(last)
    third(0)
    second(1)
    third(last)
    for i in range(2, last):
        first(i)
        third(i - 1)
        second(i)
    third(last - 1)

    for i in range(chunks):
        stores[i].wait()
    for copy in started:
        copy.wait_send()
    near_g.finish()
    wt_g.finish()


def per_device(
    incident, sources, tree_order, near_quad, near_owner, near_slot, leaf_inverse, basis_v, basis_w
):
    leaf, cols = incident.shape
    near = near_quad.shape[0]
    rank = basis_v.shape[2]
    group = lax.axis_size("col")
    rows = leaf // group
    chunks = cols // LANES
    width = leaf + 6 * rank
    vmem, sem = pltpu.VMEM, pltpu.SemaphoreType.DMA

    def f32(*shape):
        return vmem(shape, F32)

    def pair(*shape):
        return [vmem(shape, BF16), vmem(shape, BF16)]

    scratch = [
        vmem((1, leaf), jnp.int32), vmem((1, near), jnp.int32), vmem((1, near), jnp.int32),
        f32(rows, leaf), f32(2, rows, rank), f32(2, 2, rows, rank),
        f32(near, leaf), f32(leaf, cols), f32(leaf, cols),
        f32(group, near // group, leaf), f32(group, rows, width),
        vmem((8, near), jnp.int32), vmem((8, near), jnp.int32),
        f32(chunks, leaf, LANES), f32(chunks, leaf, LANES), f32(chunks, leaf, LANES),
        f32(chunks, 2 * rank, LANES), f32(chunks, 2 * rank, LANES),
        f32(chunks, rank, LANES), f32(chunks, rank, LANES),
        f32(leaf, LANES), f32(leaf, LANES), f32(leaf, LANES), f32(leaf, LANES),
        f32(rank, 2 * rank), f32(rank, 2 * rank), f32(leaf, cols),
        *pair(near, leaf), vmem((chunks, leaf, 2 * LANES), BF16), vmem((chunks, near, 2 * LANES), BF16),
        vmem((6, leaf, near), BF16), vmem((leaf, leaf), BF16),
        *pair(2 * rank, leaf), *pair(2 * rank, leaf),
        *pair(leaf, leaf + 4 * rank), *pair(leaf, leaf + 4 * rank),
        *pair(rank, 2 * rank), vmem((leaf, 2 * LANES), BF16), vmem((2 * rank, 2 * LANES), BF16),
        sem((2, 32)), sem((2, 32)), sem((4, chunks)), sem((4, chunks)), sem((5,)), sem((5,)),
        sem((9,)), sem((chunks,)),
    ]
    in_any = pl.BlockSpec(memory_space=pl.ANY)
    return pl.pallas_call(
        kernel,
        out_shape=jax.ShapeDtypeStruct((leaf, cols), F32),
        in_specs=[in_any] * 9,
        out_specs=in_any,
        scratch_shapes=scratch,
        compiler_params=pltpu.CompilerParams(
            collective_id=0, has_side_effects=True, vmem_limit_bytes=60 * 1024 * 1024
        ),
        cost_estimate=pl.CostEstimate(flops=15 * 10**9, bytes_accessed=12 * 10**6, transcendentals=0),
    )(
        tree_order, near_owner.reshape(1, near), near_slot.reshape(1, near),
        leaf_inverse, basis_v, basis_w, incident, sources, near_quad,
    )


def solution(mesh):
    placed = (
        P("leaf", "col"),
        P("leaf", "col"),
        P("leaf", None),
        P("leaf", None),
        P("leaf", None),
        P("leaf"),
        P(("leaf", "col"), None),
        P(None, ("leaf", "col"), None),
        P(None, None, ("leaf", "col"), None),
    )
    return jax.shard_map(
        per_device, mesh=mesh, in_specs=placed, out_specs=P("leaf", "col"), check_vma=False
    )
```

time: 88.1 us -> 77.7 us (0.88)
  Pallas kernels: 85.2 us -> 74.9 us
    pallas_call x1, Pallas kernels: 85.2 us -> 74.9 us  [per_device(): pl.pallas_call(kernel, out_shape=jax.ShapeDtypeStruct((leaf, cols), F32),...]
where the time goes in v2:
time: 77.7 us; the launch traced here: 77.6 us
  Pallas kernels  74.9 us (96%)
  local copies, waits for them, and re-layouts  2.67 us (3%)
    pallas_call x1, Pallas kernels, per_device(): pl.pallas_call(kernel, out_shape=jax.ShapeDtypeStruct((leaf, cols), F32),...  74.9 us
    unnamed x1, local copies, waits for them, and re-layouts  2.67 us

profile of v2, /device:TPU:0, one launch (start us, length us, event | category | flops | bytes accessed | tf_op | source)
XLA Modules:
  0.0 77.6 jit_solution(10139781433575239218)
XLA Ops:
  0.0 74.9 %shard_map.91 = f32[768,512]{1,0:T(8,128)} custom-call(s32[1,768]{1,0:T(1,128)} %tree_any.1, s32[1,1024]{1,0:T(1,128)} %bitcast.2, s32[1,1024]{1,0:T(1,128)} %bitcast.3, f32[24,768]{1,0:T(8,128)} %inverse_any.1, f32[2,24,128]{2,1,0:T(8,128)} %basis_v_any.1, f32[2,2,24,128]{3,2,1,0:T(8,128)} %basis_w_any.1, f32[768,512]{1,0:T(8,128)} %incident.1, ...), custom_call_target="tpu_custom_call" | custom-call | flops 15000000512 | bytes 12000000 | tf_op jit(solution)/shard_map/pallas_call | solution.py:519
  74.9 2.7 %copy.11 = f32[768,512]{1,0:T(8,128)} copy(f32[768,512]{1,0:T(8,128)} %shard_map.91) | data formatting | bytes 3145728

commit v3 on v2

--- a/solution.py
+++ b/solution.py
@@ -105,9 +105,8 @@
         self.send(own, 1, self.p.left1)
         self.send(own, 2, self.p.opposite1)
 
-    def ring1_end(self):
-        for sem, off1 in enumerate((3, 1, 2)):
-            self.recv(self.piece(0, off1), sem)
+    def ring1_recv(self, off1):
+        self.recv(self.piece(0, off1), (3, 1, 2).index(off1))
 
     def ring2(self, off1):
         self.send(self.piece(0, off1), 4 + off1, self.p.right2)
@@ -115,10 +114,10 @@
 
     def ring2_pass(self, off1):
         self.recv(self.piece(3, off1), 4 + off1)
-        if off1 in (0, 3):
+        if off1 in (0, 1):
             self.send(self.piece(3, off1), 12 + off1, self.p.right2)
         self.recv(self.piece(1, off1), 8 + off1)
-        if off1 in (1, 2):
+        if off1 in (3, 2):
             self.send(self.piece(1, off1), 12 + off1, self.p.left2)
 
     def ring2_end(self, off1):
@@ -143,17 +142,19 @@
     tree, owner, slot, inverse, basis_v, basis_w,
     nq, s_own, x, nqp, wt, key_out, key_in, s_in, y_out, y_in, z_out, z_in, t_out, t_in, u_out, u_in, w_out, w_in,
     m_out, m_in, acc,
-    nq_hi, nq_lo, s_hl, p_hl, oh, gt, vt_hi, vt_lo, b_hi, b_lo, ws_hi, ws_lo, wall_hi, wall_lo,
-    k_hi, k_lo, x_hl, c_hl,
+    nq_hi, nq_lo, s_hl, p_hl, oh, gt, vt_hi, vt_lo, b_hi, b_lo, ws_hi, ws_lo, wn_hi, wn_lo,
+    k_hi, k_lo, x_hl, c_hl, st_hl, nat,
     gsend, grecv, csend, crecv, osend, orecv, load_sem, out_sem,
 ):
     leaf, cols = incident.shape
     near = near_quad.shape[0]
     rank = basis_v.shape[2]
-    part = near // nqp.shape[0]
+    part = nqp.shape[2]
+    group = nqp.shape[1]
     chunks = cols // LANES
     last = chunks - 1
     near_tile, leaf_tile = near // 2, leaf // 2
+    row_parts = (pl.ds(0, 2 * leaf // 3), pl.ds(2 * leaf // 3, leaf // 3))
     place = Place()
     mine = place.col
     started = []
@@ -184,8 +185,8 @@
         started.append(copy)
         return copy
 
-    near_g = Gather(place, nqp, gsend.at[0], grecv.at[0])
-    wt_g = Gather(place, wt, gsend.at[1], grecv.at[1])
+    near_gs = [Gather(place, nqp.at[h], gsend.at[h], grecv.at[h]) for h in range(2)]
+    wt_g = Gather(place, wt, gsend.at[2], grecv.at[2])
 
     def make_gt(rows):
         number = rows.start + lax.broadcasted_iota(jnp.int32, (rows.size, leaf), 0)
@@ -203,11 +204,11 @@
     def split_near(rows):
         nq_hi[rows, :], nq_lo[rows, :] = halves(nq[rows, :])
 
+    def partial_rows(i, rows):
+        p_hl[i, rows, :] = beside(dot_beside(nq_hi[rows, :], nq_lo[rows, :], s_hl[i]))
+
     def partial(i):
-        def body(rows):
-            p_hl[i, rows, :] = beside(dot_beside(nq_hi[rows, :], nq_lo[rows, :], s_hl[i]))
-
-        tiles(near, near_tile, body)
+        tiles(near, near_tile, lambda rows: partial_rows(i, rows))
 
     def own_partial(i):
         def body(rows):
@@ -221,7 +222,7 @@
 
     for copy in loads[:6]:
         copy.wait()
-    key_out[...] = jnp.broadcast_to(owner[...] * leaf + slot[...], key_out.shape)
+    key_out[...] = owner[...] * leaf + slot[...]
     tiles(leaf, LANES, make_gt)
     nt = (((1,), (1,)), ((), ()))
     top, low = halves(inverse[...])
@@ -242,21 +243,28 @@
     pl.semaphore_wait(barrier, len(neighbours))
 
     once, per = (osend, orecv), (csend, crecv)
-    rows_mine = pl.ds(pl.multiple_of(mine * part, part), part)
-    near_swap = send(near_quad.at[rows_mine], nqp.at[mine], once, 0, place.mate)
-    key_swap = send(key_out, key_in, once, 1, place.mate)
+    near_swaps = [
+        send(
+            near_quad.at[pl.ds(pl.multiple_of(h * near // 2 + mine * part, part), part)], nqp.at[h, mine],
+            once, h, place.mate,
+        )
+        for h in range(2)
+    ]
+    key_swap = send(key_out, key_in, once, 2, place.mate)
     wt_g.ring1()
     wt_g.ring2(0)
-    wt_g.to_twin(0, 0)
     source_swaps = [
         send(sources.at[:, lane(i)], s_in.at[i], per, (0, i), place.mate) for i in range(last)
     ]
 
-    def last_across(rows):
-        y_out[last, rows, :] = sums(1, last, rows)
-
-    tiles(leaf, leaf_tile, last_across)
-    sum_swaps = {last: send(y_out.at[last], y_in.at[last], per, (1, last), place.cross)}
+    def send_sums(i, part):
+        rows = row_parts[part]
+        return send(y_out.at[i, rows], y_in.at[i, rows], per, (1 + 3 * part, i), place.cross)
+
+    sum_swaps = {last: []}
+    for k in range(2):
+        y_out[last, row_parts[k], :] = sums(1, last, row_parts[k])
+        sum_swaps[last].append(send_sums(last, k))
 
     def last_far(rows):
         w_out[rows, :] = sums(3, last, rows)
@@ -265,22 +273,26 @@
     far_swap = send(w_out, w_in, once, 3, place.cross)
     make_one_hot(2, key_out, place.mate[0])
     make_one_hot(0, key_out, place.leaf)
-
-    near_swap.wait_recv()
-    near_g.ring1()
-    near_g.ring2(0)
-    near_g.to_twin(0, 0)
-
-    for i in range(last):
+    own_partial(0)
+
+    for h in range(2):
+        near_swaps[h].wait_recv()
+        near_gs[h].ring1()
+        near_gs[h].ring2(0)
+    wt_g.ring1_recv(3)
+    wt_g.ring2(3)
+    for g in (*near_gs, wt_g):
+        g.to_twin(0, 0)
+    for i in range(1, last):
         own_partial(i)
-    near_g.ring1_end()
-    for off1 in (3, 1, 2):
-        near_g.ring2(off1)
-    for off1 in (3, 1, 2):
-        near_g.to_twin(0, off1)
-    wt_g.ring1_end()
-    for off1 in (3, 1, 2):
-        wt_g.to_twin(0, off1)
+    for g in near_gs:
+        for off1 in (3, 1, 2):
+            g.ring1_recv(off1)
+            g.ring2(off1)
+    for g in near_gs:
+        g.ring2_pass(0)
+        for off1 in (3, 1, 2):
+            g.to_twin(0, off1)
     loads[8].wait()
 
     def own_sums(i):
@@ -296,29 +308,41 @@
     own_sums(last)
     for i in range(last // 2):
         own_sums(i)
+    wt_g.ring1_recv(1)
+    wt_g.ring1_recv(2)
+    for g in near_gs:
+        for off1 in (3, 1, 2):
+            g.ring2_pass(off1)
+    wt_g.ring2(1)
+    wt_g.ring2(2)
+    wt_g.ring2_pass(0)
+    wt_g.ring2_pass(3)
     for off1 in (0, 3, 1, 2):
-        near_g.ring2_pass(off1)
-    for off1 in (3, 1, 2):
-        wt_g.ring2(off1)
-    for off1 in (0, 3, 1, 2):
-        near_g.to_twin(3, off1)
-        near_g.to_twin(1, off1)
+        for g in near_gs:
+            g.to_twin(3, off1)
+            g.to_twin(1, off1)
     for i in range(last // 2, last):
         own_sums(i)
     key_swap.wait_recv()
     make_one_hot(4, key_in, place.leaf)
     make_one_hot(5, key_in, place.cross[0])
-    for off1 in (0, 3, 1, 2):
-        near_g.ring2_end(off1)
-        near_g.to_twin(2, off1)
-    near_g.from_twin()
-
-    def split_partner(index, carry):
-        rows = pl.ds(pl.multiple_of(index * 2 * part, 2 * part), 2 * part)
-        nq_hi[rows, :], nq_lo[rows, :] = halves(nqp[pl.ds(2 * index, 2)].reshape(2 * part, leaf))
-        return carry
-
-    lax.fori_loop(0, nqp.shape[0] // 2, split_partner, 0)
+    for g in near_gs:
+        for off1 in (0, 3, 1, 2):
+            g.ring2_end(off1)
+            g.to_twin(2, off1)
+    for off1 in (3, 1, 2):
+        wt_g.to_twin(0, off1)
+
+    def split_partner(h):
+        count = 4 * part
+
+        def body(index, carry):
+            rows = pl.ds(pl.multiple_of(h * near // 2 + index * count, count), count)
+            block = nqp[h, pl.ds(4 * index, 4)].reshape(count, leaf)
+            nq_hi[rows, :], nq_lo[rows, :] = halves(block)
+            return carry
+
+        lax.fori_loop(0, group // 4, body, 0)
 
     z_swaps, t_swaps, stores = {}, {}, {}
 
@@ -329,13 +353,17 @@
             s_hl[i, rows, :] = beside(s_in[i, rows, :])
 
         tiles(leaf, LANES, split)
-        partial(i)
-
-        def across(rows):
-            y_out[i, rows, :] += sums(5, i, rows)
-
-        tiles(leaf, leaf_tile, across)
-        sum_swaps[i] = send(y_out.at[i], y_in.at[i], per, (1, i), place.cross)
+        if i == 0:
+            for h in range(2):
+                near_gs[h].from_twin()
+                split_partner(h)
+                partial_rows(i, pl.ds(h * near // 2, near // 2))
+        else:
+            partial(i)
+        sum_swaps[i] = []
+        for k in range(2):
+            y_out[i, row_parts[k], :] += sums(5, i, row_parts[k])
+            sum_swaps[i].append(send_sums(i, k))
 
         def here(rows):
             x[rows, lane(i)] += sums(4, i, rows)
@@ -368,22 +396,29 @@
         second_v = pl.ds(rank, rank)
         first_w = pl.ds(leaf, 2 * rank)
         m_out[...] = dot3(vt_hi[second_v, :], vt_lo[second_v, :], ws_hi[:, first_w], ws_lo[:, first_w])
-        swap = send(m_out, m_in, once, 2, place.mate)
+        mine_m = half_m()
+        swap = send(m_out.at[mine_m], m_in.at[mine_m], once, 5, place.mate)
         step = min(256, leaf)
         for k in range(leaf // step):
             block = pl.ds(k * step, step)
             r = dot3(vt_hi[...], vt_lo[...], ws_hi[:, block], ws_lo[:, block])
             b_hi[:, block], b_lo[:, block] = halves(r)
-        for k in range((leaf + 4 * rank) // step):
-            block = pl.ds(k * step, step)
-            sign = 1.0 if k * step < leaf else -1.0
-
-            def body(rows):
-                wall_hi[rows, block] = (dot(gt[rows, :], ws_hi[:, block]) * sign).astype(BF16)
-                wall_lo[rows, block] = (dot(gt[rows, :], ws_lo[:, block]) * sign).astype(BF16)
-
-            tiles(leaf, leaf_tile, body)
+        sibling = pl.ds(leaf + 2 * rank, rank)
+
+        def body(rows):
+            wn_hi[rows, :] = dot(gt[rows, :], ws_hi[:, sibling]).astype(BF16)
+            wn_lo[rows, :] = dot(gt[rows, :], ws_lo[:, sibling]).astype(BF16)
+
+        tiles(leaf, leaf_tile, body)
         return swap
+
+    def half_m():
+        return pl.ds(pl.multiple_of(place.core * (rank // 2), rank // 2), rank // 2)
+
+    def corrections_pass(swap):
+        swap.wait_recv()
+        ref = m_in.at[half_m()]
+        return send(ref, ref, once, 6, place.twin)
 
     def corrections(swap):
         swap.wait_recv()
@@ -393,19 +428,19 @@
 
     def apply(rows, at, size, value):
         block = pl.ds(at, size)
-        return dot_beside(wall_hi[rows, block], wall_lo[rows, block], value)
+        return dot_beside(ws_hi[rows, block], ws_lo[rows, block], value)
 
     def first(i, more=None):
-        sum_swaps[i].wait_recv()
         if more is not None:
             more.wait_recv()
-
-        def split(rows):
+        z = None
+        for k, rows in enumerate(row_parts):
+            sum_swaps[i][k].wait_recv()
             whole = x[rows, lane(i)] + y_in[i, rows, :]
             x_hl[rows, :] = beside(whole if more is None else whole + u_in[rows, :])
-
-        tiles(leaf, LANES, split)
-        z_out[i] = dot_beside(b_hi[...], b_lo[...], x_hl[...])
+            term = dot_beside(b_hi[:, rows], b_lo[:, rows], x_hl[rows, :])
+            z = term if z is None else z + term
+        z_out[i] = z
         z_swaps[i] = send(z_out.at[i], z_in.at[i], per, (2, i), place.mate)
 
         def state(rows):
@@ -424,26 +459,31 @@
         t_hl = beside(total)
 
         def update(rows):
-            acc[rows, lane(i)] += apply(rows, leaf, 2 * rank, c_hl[...]) + apply(
-                rows, leaf + 3 * rank, rank, t_hl
-            )
+            change = apply(rows, leaf, 2 * rank, c_hl[...]) + apply(rows, leaf + 3 * rank, rank, t_hl)
+            st_hl[rows, :] = beside(acc[rows, lane(i)] - change)
 
         tiles(leaf, leaf_tile, update)
+
+        def natural(rows):
+            nat[rows, lane(i)] = fold(dot(gt[rows, :], st_hl[...]))
+
+        tiles(leaf, leaf_tile, natural)
 
     def third(i):
         t_swaps[i].wait_recv()
         t_hl = beside(t_in[i])
 
         def update(rows):
-            acc[rows, lane(i)] += apply(rows, leaf + 2 * rank, rank, t_hl)
+            nat[rows, lane(i)] -= dot_beside(wn_hi[rows, :], wn_lo[rows, :], t_hl)
 
         tiles(leaf, leaf_tile, update)
-        stores[i] = pltpu.make_async_copy(acc.at[:, lane(i)], out.at[:, lane(i)], out_sem.at[i])
+        stores[i] = pltpu.make_async_copy(nat.at[:, lane(i)], out.at[:, lane(i)], out_sem.at[i])
         stores[i].start()
 
     near_chunk(0)
+    for off1 in (1, 2):
+        wt_g.ring2_pass(off1)
     for off1 in (0, 3, 1, 2):
-        wt_g.ring2_pass(off1)
         wt_g.to_twin(3, off1)
         wt_g.to_twin(1, off1)
     near_chunk(1)
@@ -456,26 +496,28 @@
     wt_g.from_twin()
     m_swap = weights()
     first(0)
+    first(last, mate_sums)
+    m_swap = corrections_pass(m_swap)
+    first(1)
     corrections(m_swap)
-    first(last, mate_sums)
     second(0)
-    first(1)
     second(last)
+    second(1)
     third(0)
-    second(1)
+    for i in range(2, last):
+        first(i)
     third(last)
     for i in range(2, last):
-        first(i)
-        third(i - 1)
         second(i)
-    third(last - 1)
+    for i in range(1, last):
+        third(i)
 
     for i in range(chunks):
         stores[i].wait()
     for copy in started:
         copy.wait_send()
-    near_g.finish()
-    wt_g.finish()
+    for g in (*near_gs, wt_g):
+        g.finish()
 
 
 def per_device(
@@ -500,8 +542,8 @@
         vmem((1, leaf), jnp.int32), vmem((1, near), jnp.int32), vmem((1, near), jnp.int32),
         f32(rows, leaf), f32(2, rows, rank), f32(2, 2, rows, rank),
         f32(near, leaf), f32(leaf, cols), f32(leaf, cols),
-        f32(group, near // group, leaf), f32(group, rows, width),
-        vmem((8, near), jnp.int32), vmem((8, near), jnp.int32),
+        f32(2, group, near // (2 * group), leaf), f32(group, rows, width),
+        vmem((1, near), jnp.int32), vmem((1, near), jnp.int32),
         f32(chunks, leaf, LANES), f32(chunks, leaf, LANES), f32(chunks, leaf, LANES),
         f32(chunks, 2 * rank, LANES), f32(chunks, 2 * rank, LANES),
         f32(chunks, rank, LANES), f32(chunks, rank, LANES),
@@ -510,9 +552,10 @@
         *pair(near, leaf), vmem((chunks, leaf, 2 * LANES), BF16), vmem((chunks, near, 2 * LANES), BF16),
         vmem((6, leaf, near), BF16), vmem((leaf, leaf), BF16),
         *pair(2 * rank, leaf), *pair(2 * rank, leaf),
-        *pair(leaf, leaf + 4 * rank), *pair(leaf, leaf + 4 * rank),
+        *pair(leaf, leaf + 4 * rank), *pair(leaf, rank),
         *pair(rank, 2 * rank), vmem((leaf, 2 * LANES), BF16), vmem((2 * rank, 2 * LANES), BF16),
-        sem((2, 32)), sem((2, 32)), sem((4, chunks)), sem((4, chunks)), sem((5,)), sem((5,)),
+        vmem((leaf, 2 * LANES), BF16), f32(leaf, cols),
+        sem((3, 32)), sem((3, 32)), sem((5, chunks)), sem((5, chunks)), sem((7,)), sem((7,)),
         sem((9,)), sem((chunks,)),
     ]
     in_any = pl.BlockSpec(memory_space=pl.ANY)

time: 77.7 us -> 76.7 us (0.987)
  Pallas kernels: 74.9 us -> 73.2 us
    pallas_call x1, Pallas kernels: 74.9 us -> 73.2 us  [per_device(): pl.pallas_call(kernel, out_shape=jax.ShapeDtypeStruct((leaf, cols), F32),...]
where the time goes in v3:
time: 76.7 us; the launch traced here: 75.9 us
  Pallas kernels  73.2 us (95%)
  local copies, waits for them, and re-layouts  2.67 us (3%)
    pallas_call x1, Pallas kernels, per_device(): pl.pallas_call(kernel, out_shape=jax.ShapeDtypeStruct((leaf, cols), F32),...  73.2 us
    unnamed x1, local copies, waits for them, and re-layouts  2.67 us

profile of v3, /device:TPU:0, one launch (start us, length us, event | category | flops | bytes accessed | tf_op | source)
XLA Modules:
  0.0 75.9 jit_solution(13899018878189261571)
XLA Ops:
  0.0 73.2 %shard_map.91 = f32[768,512]{1,0:T(8,128)} custom-call(s32[1,768]{1,0:T(1,128)} %tree_any.1, s32[1,1024]{1,0:T(1,128)} %bitcast.2, s32[1,1024]{1,0:T(1,128)} %bitcast.3, f32[24,768]{1,0:T(8,128)} %inverse_any.1, f32[2,24,128]{2,1,0:T(8,128)} %basis_v_any.1, f32[2,2,24,128]{3,2,1,0:T(8,128)} %basis_w_any.1, f32[768,512]{1,0:T(8,128)} %incident.1, ...), custom_call_target="tpu_custom_call" | custom-call | flops 15000000512 | bytes 12000000 | tf_op jit(solution)/shard_map/pallas_call | solution.py:562
  73.2 2.7 %copy.11 = f32[768,512]{1,0:T(8,128)} copy(f32[768,512]{1,0:T(8,128)} %shard_map.91) | data formatting | bytes 3145728

commit v4 on v3

--- a/solution.py
+++ b/solution.py
@@ -63,7 +63,7 @@
         self.right1 = (self.leaf, self.index(self.core, 0, 1))
         self.left1 = (self.leaf, self.index(self.core, 0, RING - 1))
         self.opposite1 = (self.leaf, self.index(self.core, 0, 2))
-        self.far = self.leaf + 2 - 4 * (self.leaf // 2)
+        self.far = (self.leaf + 2 - 4 * (self.leaf // 2), self.col)
         self.right2 = (self.leaf, self.index(self.core, 1, 0))
         self.left2 = (self.leaf, self.index(self.core, RING - 1, 0))
 
@@ -138,13 +138,13 @@
 
 
 def kernel(
-    tree_any, owner_any, slot_any, inverse_any, basis_v_any, basis_w_any, incident, sources, near_quad, out,
+    tree_any, owner_any, slot_any, inverse_any, basis_v_any, basis_w_any, incident, sources, near_quad, nat,
     tree, owner, slot, inverse, basis_v, basis_w,
     nq, s_own, x, nqp, wt, key_out, key_in, s_in, y_out, y_in, z_out, z_in, t_out, t_in, u_out, u_in, w_out, w_in,
-    m_out, m_in, acc,
+    m_out, m_in, far_in,
     nq_hi, nq_lo, s_hl, p_hl, oh, gt, vt_hi, vt_lo, b_hi, b_lo, ws_hi, ws_lo, wn_hi, wn_lo,
-    k_hi, k_lo, x_hl, c_hl, st_hl, nat,
-    gsend, grecv, csend, crecv, osend, orecv, load_sem, out_sem,
+    k_hi, k_lo, x_hl, c_hl, st_hl,
+    gsend, grecv, csend, crecv, osend, orecv, load_sem,
 ):
     leaf, cols = incident.shape
     near = near_quad.shape[0]
@@ -169,7 +169,8 @@
     loads = [pltpu.make_async_copy(src, dst, load_sem.at[i]) for i, (src, dst) in enumerate(pairs)]
     barrier = pltpu.get_barrier_semaphore()
     neighbours = (
-        place.mate, place.cross, place.twin, place.right1, place.left1, place.opposite1, place.right2, place.left2
+        place.mate, place.cross, place.far, place.twin, place.right1, place.left1, place.opposite1, place.right2,
+        place.left2,
     )
     for device in neighbours:
         pl.semaphore_signal(barrier, inc=1, device_id=device, device_id_type=MESH)
@@ -234,7 +235,7 @@
     for k in range(2):
         wt[mine, :, pl.ds(leaf + (4 + k) * rank, rank)] = basis_v[k]
     make_one_hot(1, key_out, place.cross[0])
-    make_one_hot(3, key_out, place.far)
+    make_one_hot(3, key_out, place.far[0])
     loads[6].wait()
     tiles(near, LANES, split_near)
     loads[7].wait()
@@ -252,7 +253,6 @@
     ]
     key_swap = send(key_out, key_in, once, 2, place.mate)
     wt_g.ring1()
-    wt_g.ring2(0)
     source_swaps = [
         send(sources.at[:, lane(i)], s_in.at[i], per, (0, i), place.mate) for i in range(last)
     ]
@@ -274,25 +274,6 @@
     make_one_hot(2, key_out, place.mate[0])
     make_one_hot(0, key_out, place.leaf)
     own_partial(0)
-
-    for h in range(2):
-        near_swaps[h].wait_recv()
-        near_gs[h].ring1()
-        near_gs[h].ring2(0)
-    wt_g.ring1_recv(3)
-    wt_g.ring2(3)
-    for g in (*near_gs, wt_g):
-        g.to_twin(0, 0)
-    for i in range(1, last):
-        own_partial(i)
-    for g in near_gs:
-        for off1 in (3, 1, 2):
-            g.ring1_recv(off1)
-            g.ring2(off1)
-    for g in near_gs:
-        g.ring2_pass(0)
-        for off1 in (3, 1, 2):
-            g.to_twin(0, off1)
     loads[8].wait()
 
     def own_sums(i):
@@ -305,32 +286,49 @@
 
         tiles(leaf, leaf_tile, body)
 
+    for g, swap in zip(near_gs, near_swaps):
+        swap.wait_recv()
+        g.ring1()
+        g.ring2(0)
+        g.to_twin(0, 0)
+    own_partial(1)
     own_sums(last)
-    for i in range(last // 2):
-        own_sums(i)
-    wt_g.ring1_recv(1)
-    wt_g.ring1_recv(2)
     for g in near_gs:
         for off1 in (3, 1, 2):
-            g.ring2_pass(off1)
-    wt_g.ring2(1)
-    wt_g.ring2(2)
-    wt_g.ring2_pass(0)
-    wt_g.ring2_pass(3)
-    for off1 in (0, 3, 1, 2):
-        for g in near_gs:
+            g.ring1_recv(off1)
+            g.ring2(off1)
+        g.ring2_pass(0)
+    for g in near_gs:
+        for off1 in (3, 1, 2):
+            g.to_twin(0, off1)
+    own_sums(0)
+    for i in range(2, last):
+        own_partial(i)
+    for off1 in (3, 1, 2):
+        near_gs[0].ring2_pass(off1)
+    own_sums(1)
+    for off1 in (3, 1, 2):
+        near_gs[1].ring2_pass(off1)
+    wt_g.ring2(0)
+    for off1 in (3, 1, 2):
+        wt_g.ring1_recv(off1)
+        wt_g.ring2(off1)
+    for g in near_gs:
+        for off1 in (0, 3, 1, 2):
             g.to_twin(3, off1)
             g.to_twin(1, off1)
-    for i in range(last // 2, last):
+    key_swap.wait_recv()
+    make_one_hot(5, key_in, place.cross[0])
+    make_one_hot(4, key_in, place.leaf)
+    for off1 in (0, 3, 1, 2):
+        near_gs[0].ring2_end(off1)
+        near_gs[0].to_twin(2, off1)
+    for i in range(2, last):
         own_sums(i)
-    key_swap.wait_recv()
-    make_one_hot(4, key_in, place.leaf)
-    make_one_hot(5, key_in, place.cross[0])
-    for g in near_gs:
-        for off1 in (0, 3, 1, 2):
-            g.ring2_end(off1)
-            g.to_twin(2, off1)
-    for off1 in (3, 1, 2):
+    for off1 in (0, 3, 1, 2):
+        near_gs[1].ring2_end(off1)
+        near_gs[1].to_twin(2, off1)
+    for off1 in (0, 3, 1, 2):
         wt_g.to_twin(0, off1)
 
     def split_partner(h):
@@ -344,7 +342,7 @@
 
         lax.fori_loop(0, group // 4, body, 0)
 
-    z_swaps, t_swaps, stores = {}, {}, {}
+    z_swaps, t_swaps = {}, {}
 
     def near_chunk(i):
         source_swaps[i].wait_recv()
@@ -403,13 +401,14 @@
             block = pl.ds(k * step, step)
             r = dot3(vt_hi[...], vt_lo[...], ws_hi[:, block], ws_lo[:, block])
             b_hi[:, block], b_lo[:, block] = halves(r)
-        sibling = pl.ds(leaf + 2 * rank, rank)
-
-        def body(rows):
-            wn_hi[rows, :] = dot(gt[rows, :], ws_hi[:, sibling]).astype(BF16)
-            wn_lo[rows, :] = dot(gt[rows, :], ws_lo[:, sibling]).astype(BF16)
-
-        tiles(leaf, leaf_tile, body)
+        for k in range(2):
+            block, source = pl.ds(2 * k * rank, 2 * rank), pl.ds(leaf + 2 * k * rank, 2 * rank)
+
+            def body(rows):
+                wn_hi[rows, block] = dot(gt[rows, :], ws_hi[:, source]).astype(BF16)
+                wn_lo[rows, block] = dot(gt[rows, :], ws_lo[:, source]).astype(BF16)
+
+            tiles(leaf, leaf_tile, body)
         return swap
 
     def half_m():
@@ -426,9 +425,12 @@
         k_hi[:, one], k_lo[:, one] = halves(m_out[:, one] + m_in[:, two])
         k_hi[:, two], k_lo[:, two] = halves(m_out[:, two] + m_in[:, one])
 
-    def apply(rows, at, size, value):
-        block = pl.ds(at, size)
-        return dot_beside(ws_hi[rows, block], ws_lo[rows, block], value)
+    one, two = pl.ds(0, rank), pl.ds(rank, rank)
+    state_columns = pl.ds(0, leaf)
+
+    def correct(rows, i, at, size):
+        block = pl.ds(at * rank, size * rank)
+        nat[rows, lane(i)] -= dot_beside(wn_hi[rows, block], wn_lo[rows, block], c_hl[block, :])
 
     def first(i, more=None):
         if more is not None:
@@ -441,58 +443,69 @@
             term = dot_beside(b_hi[:, rows], b_lo[:, rows], x_hl[rows, :])
             z = term if z is None else z + term
         z_out[i] = z
+        if i == direct:
+            own = beside(z_out[i, one, :])
+            z_out[i, two, :] = z_out[i, two, :] - dot_beside(k_hi[:, two], k_lo[:, two], own)
+            far_swaps.append(send(z_out.at[i, two], far_in, once, 7, place.far))
+            t_swaps[i] = send(z_out.at[i, two], t_in.at[i], per, (3, i), place.cross)
         z_swaps[i] = send(z_out.at[i], z_in.at[i], per, (2, i), place.mate)
 
         def state(rows):
-            acc[rows, lane(i)] = apply(rows, 0, leaf, x_hl[...])
+            st_hl[rows, :] = beside(dot_beside(ws_hi[rows, state_columns], ws_lo[rows, state_columns], x_hl[...]))
 
         tiles(leaf, leaf_tile, state)
+
+        def natural(rows):
+            nat[rows, lane(i)] = fold(dot(gt[rows, :], st_hl[...]))
+
+        tiles(leaf, leaf_tile, natural)
 
     def second(i):
         z_swaps[i].wait_recv()
-        one, two = pl.ds(0, rank), pl.ds(rank, rank)
         c_hl[one, :] = beside(z_in[i, one, :])
         c_hl[two, :] = beside(z_out[i, one, :])
-        total = z_out[i, two, :] + z_in[i, two, :] - dot_beside(k_hi[...], k_lo[...], c_hl[...])
+        both = pl.ds(0, 2 * rank)
+        total = z_out[i, two, :] + z_in[i, two, :] - dot_beside(k_hi[...], k_lo[...], c_hl[both, :])
         t_out[i] = total
         t_swaps[i] = send(t_out.at[i], t_in.at[i], per, (3, i), place.cross)
-        t_hl = beside(total)
+        c_hl[pl.ds(3 * rank, rank), :] = beside(total)
 
         def update(rows):
-            change = apply(rows, leaf, 2 * rank, c_hl[...]) + apply(rows, leaf + 3 * rank, rank, t_hl)
-            st_hl[rows, :] = beside(acc[rows, lane(i)] - change)
+            correct(rows, i, 0, 2)
+            correct(rows, i, 3, 1)
 
         tiles(leaf, leaf_tile, update)
-
-        def natural(rows):
-            nat[rows, lane(i)] = fold(dot(gt[rows, :], st_hl[...]))
-
-        tiles(leaf, leaf_tile, natural)
 
     def third(i):
         t_swaps[i].wait_recv()
-        t_hl = beside(t_in[i])
-
-        def update(rows):
-            nat[rows, lane(i)] -= dot_beside(wn_hi[rows, :], wn_lo[rows, :], t_hl)
-
-        tiles(leaf, leaf_tile, update)
-        stores[i] = pltpu.make_async_copy(nat.at[:, lane(i)], out.at[:, lane(i)], out_sem.at[i])
-        stores[i].start()
-
+        c_hl[pl.ds(2 * rank, rank), :] = beside(t_in[i])
+        tiles(leaf, leaf_tile, lambda rows: correct(rows, i, 2, 1))
+
+    def at_once(i):
+        z_swaps[i].wait_recv()
+        c_hl[one, :] = beside(z_in[i, one, :])
+        c_hl[two, :] = beside(z_out[i, one, :])
+        c_hl[pl.ds(3 * rank, rank), :] = beside(z_out[i, two, :] + z_in[i, two, :])
+        t_swaps[i].wait_recv()
+        far_swaps[0].wait_recv()
+        c_hl[pl.ds(2 * rank, rank), :] = beside(t_in[i] + far_in[...])
+        tiles(leaf, leaf_tile, lambda rows: correct(rows, i, 0, 4))
+
+    direct = last - 1
+    far_swaps = []
     near_chunk(0)
-    for off1 in (1, 2):
+    near_chunk(1)
+    mate_sums = pass_on()
+    for off1 in (0, 3, 1, 2):
         wt_g.ring2_pass(off1)
     for off1 in (0, 3, 1, 2):
         wt_g.to_twin(3, off1)
         wt_g.to_twin(1, off1)
-    near_chunk(1)
-    mate_sums = pass_on()
+    for i in range(2, last):
+        near_chunk(i)
     for off1 in (0, 3, 1, 2):
         wt_g.ring2_end(off1)
         wt_g.to_twin(2, off1)
-    for i in range(2, last):
-        near_chunk(i)
     wt_g.from_twin()
     m_swap = weights()
     first(0)
@@ -500,24 +513,30 @@
     m_swap = corrections_pass(m_swap)
     first(1)
     corrections(m_swap)
-    second(0)
-    second(last)
-    second(1)
-    third(0)
-    for i in range(2, last):
-        first(i)
-    third(last)
-    for i in range(2, last):
+    for i in (0, last, 1):
         second(i)
-    for i in range(1, last):
+    first(direct)
+    for i in (0, last, 1):
         third(i)
-
-    for i in range(chunks):
-        stores[i].wait()
+    at_once(direct)
+
     for copy in started:
         copy.wait_send()
     for g in (*near_gs, wt_g):
         g.finish()
+
+
+def hand_over(value, out, out_sem):
+    count = out_sem.shape[0]
+    size = value.shape[0] // count
+    copies = [
+        pltpu.make_async_copy(value.at[pl.ds(i * size, size)], out.at[pl.ds(i * size, size)], out_sem.at[i])
+        for i in range(count)
+    ]
+    for copy in copies:
+        copy.start()
+    for copy in copies:
+        copy.wait()
 
 
 def per_device(
@@ -548,31 +567,38 @@
         f32(chunks, 2 * rank, LANES), f32(chunks, 2 * rank, LANES),
         f32(chunks, rank, LANES), f32(chunks, rank, LANES),
         f32(leaf, LANES), f32(leaf, LANES), f32(leaf, LANES), f32(leaf, LANES),
-        f32(rank, 2 * rank), f32(rank, 2 * rank), f32(leaf, cols),
+        f32(rank, 2 * rank), f32(rank, 2 * rank), f32(rank, LANES),
         *pair(near, leaf), vmem((chunks, leaf, 2 * LANES), BF16), vmem((chunks, near, 2 * LANES), BF16),
         vmem((6, leaf, near), BF16), vmem((leaf, leaf), BF16),
         *pair(2 * rank, leaf), *pair(2 * rank, leaf),
-        *pair(leaf, leaf + 4 * rank), *pair(leaf, rank),
-        *pair(rank, 2 * rank), vmem((leaf, 2 * LANES), BF16), vmem((2 * rank, 2 * LANES), BF16),
-        vmem((leaf, 2 * LANES), BF16), f32(leaf, cols),
-        sem((3, 32)), sem((3, 32)), sem((5, chunks)), sem((5, chunks)), sem((7,)), sem((7,)),
-        sem((9,)), sem((chunks,)),
+        *pair(leaf, leaf + 4 * rank), *pair(leaf, 4 * rank),
+        *pair(rank, 2 * rank), vmem((leaf, 2 * LANES), BF16), vmem((4 * rank, 2 * LANES), BF16),
+        vmem((leaf, 2 * LANES), BF16),
+        sem((3, 32)), sem((3, 32)), sem((5, chunks)), sem((5, chunks)), sem((8,)), sem((8,)),
+        sem((9,)),
     ]
     in_any = pl.BlockSpec(memory_space=pl.ANY)
-    return pl.pallas_call(
+    solved = pl.pallas_call(
         kernel,
-        out_shape=jax.ShapeDtypeStruct((leaf, cols), F32),
+        out_shape=pltpu.VMEM((leaf, cols), F32),
         in_specs=[in_any] * 9,
-        out_specs=in_any,
+        out_specs=pl.BlockSpec(memory_space=pltpu.VMEM),
         scratch_shapes=scratch,
         compiler_params=pltpu.CompilerParams(
-            collective_id=0, has_side_effects=True, vmem_limit_bytes=60 * 1024 * 1024
+            collective_id=0, has_side_effects=True, vmem_limit_bytes=54 * 1024 * 1024
         ),
         cost_estimate=pl.CostEstimate(flops=15 * 10**9, bytes_accessed=12 * 10**6, transcendentals=0),
     )(
         tree_order, near_owner.reshape(1, near), near_slot.reshape(1, near),
         leaf_inverse, basis_v, basis_w, incident, sources, near_quad,
     )
+    return pl.pallas_call(
+        hand_over,
+        out_shape=jax.ShapeDtypeStruct((leaf, cols), F32),
+        in_specs=[pl.BlockSpec(memory_space=pltpu.VMEM)],
+        out_specs=in_any,
+        scratch_shapes=[sem((chunks,))],
+    )(solved)
 
 
 def solution(mesh):

time: 76.7 us -> 73 us (0.952)
  Pallas kernels: 73.2 us -> 70.8 us
  local copies, waits for them, and re-layouts: 2.67 us -> 1.15 us
    pallas_call x1 -> x2, Pallas kernels: 73.2 us -> 70.8 us  [the longest x1 68.2 us: per_device(): pl.pallas_call(kernel, out_shape=pltpu.VMEM((leaf, cols), F32), in_specs=...]
    unnamed x1 -> x2, local copies, waits for them, and re-layouts: 2.67 us -> 1.15 us
where the time goes in v4:
time: 73 us; the launch traced here: 72.1 us
  Pallas kernels  70.8 us (97%)
  local copies, waits for them, and re-layouts  1.15 us (2%)
    pallas_call x1, Pallas kernels, per_device(): pl.pallas_call(kernel, out_shape=pltpu.VMEM((leaf, cols), F32), in_specs=...  68.2 us
    pallas_call x1, Pallas kernels, per_device(): pl.pallas_call(hand_over, out_shape=jax.ShapeDtypeStruct((leaf, cols), F3...  2.57 us

profile of v4, /device:TPU:0, one launch (start us, length us, event | category | flops | bytes accessed | tf_op | source)
XLA Modules:
  0.0 72.1 jit_solution(6271554780596893342)
XLA Ops:
  0.0 68.2 %shard_map.91.value = f32[768,512]{1,0:T(8,128)S(1)} custom-call(s32[1,768]{1,0:T(1,128)} %tree_any.1, s32[1,1024]{1,0:T(1,128)} %bitcast.2, s32[1,1024]{1,0:T(1,128)} %bitcast.3, f32[24,768]{1,0:T(8,128)} %inverse_any.1, f32[2,24,128]{2,1,0:T(8,128)} %basis_v_any.1, f32[2,2,24,128]{3,2,1,0:T(8,128)} %basis_w_any.1, f32[768,512]{1,0:T(8,128)} %incident.1, ...), custom_call_target="tpu_custom_call" | custom-call | flops 15000000512 | bytes 12000000 | tf_op jit(solution)/shard_map/pallas_call | solution.py:581
  68.2 0.0 copy-start
  68.2 1.1 %copy-done = f32[768,512]{1,0:T(8,128)} copy-done((f32[768,512]{1,0:T(8,128)}, f32[768,512]{1,0:T(8,128)S(1)}, u32[]{:S(2)}) %copy-start) | copy-done | bytes 1572888
  69.3 2.6 %shard_map.92 = f32[768,512]{1,0:T(8,128)} custom-call(f32[768,512]{1,0:T(8,128)} %copy-done), custom_call_target="tpu_custom_call" | custom-call | tf_op jit(solution)/shard_map/pallas_call | solution.py:595
Async XLA Ops:
  68.2 1.2 %copy-start = (f32[768,512]{1,0:T(8,128)}, f32[768,512]{1,0:T(8,128)S(1)}, u32[]{:S(2)}) copy-start(f32[768,512]{1,0:T(8,128)S(1)} %shard_map.91.value) | copy-start | bytes 4718596

commit v5 on v4

--- a/solution.py
+++ b/solution.py
@@ -60,21 +60,28 @@
         self.twin = (self.leaf, self.col + 1 - 2 * self.core)
         self.mate = (self.leaf + 1 - 2 * (self.leaf % 2), self.col)
         self.cross = (3 - self.leaf, self.col)
-        self.right1 = (self.leaf, self.index(self.core, 0, 1))
-        self.left1 = (self.leaf, self.index(self.core, 0, RING - 1))
-        self.opposite1 = (self.leaf, self.index(self.core, 0, 2))
+        self.right1 = self.device(0, 1)
+        self.left1 = self.device(0, RING - 1)
+        self.opposite1 = self.device(0, 2)
         self.far = (self.leaf + 2 - 4 * (self.leaf // 2), self.col)
-        self.right2 = (self.leaf, self.index(self.core, 1, 0))
-        self.left2 = (self.leaf, self.index(self.core, RING - 1, 0))
-
-    def index(self, core, off2, off1):
-        a, b = (self.d2 + off2) % RING, (self.d1 + off1) % RING
-        return (a * 2 * RING + b * 2) * (1 - core) + (b * 2 * RING + a * 2 + 1) * core
+        self.right2 = self.device(1, 0)
+        self.left2 = self.device(RING - 1, 0)
+
+    def device(self, off2, off1):
+        a, b, core = (self.d2 + off2) % RING, (self.d1 + off1) % RING, self.core
+        return self.leaf, (a * 2 * RING + b * 2) * (1 - core) + (b * 2 * RING + a * 2 + 1) * core
+
+    def group(self, off2):
+        return (self.core * RING + (self.d2 + off2) % RING) * RING
+
+    def twin_group(self, off2):
+        return ((1 - self.core) * RING + (self.d1 + off2) % RING) * RING
+
+    def index(self, off2, off1):
+        return self.group(off2) + (self.d1 + off1) % RING
 
     def twin_index(self, off2, off1):
-        core = 1 - self.core
-        a, b = (self.d1 + off2) % RING, (self.d2 + off1) % RING
-        return (a * 2 * RING + b * 2) * (1 - core) + (b * 2 * RING + a * 2 + 1) * core
+        return self.twin_group(off2) + (self.d2 + off1) % RING
 
 
 class Gather:
@@ -83,7 +90,7 @@
         self.started = []
 
     def piece(self, off2, off1):
-        return self.buf.at[self.p.index(self.p.core, off2, off1)]
+        return self.buf.at[self.p.index(off2, off1)]
 
     def send(self, ref, sem, device):
         copy = pltpu.make_async_remote_copy(
@@ -123,14 +130,18 @@
     def ring2_end(self, off1):
         self.recv(self.piece(2, off1), 12 + off1)
 
-    def to_twin(self, off2, off1):
-        self.send(self.piece(off2, off1), 16 + 4 * off2 + off1, self.p.twin)
+    def to_twin(self, off2):
+        self.send(self.buf.at[pl.ds(self.p.group(off2), RING)], 16 + off2, self.p.twin)
+
+    def end_to_twin(self, off1):
+        self.ring2_end(off1)
+        self.send(self.piece(2, off1), 20 + off1, self.p.twin)
 
     def from_twin(self):
-        for off2 in range(RING):
-            for off1 in range(RING):
-                ref = self.buf.at[self.p.twin_index(off2, off1)]
-                self.recv(ref, 16 + 4 * off2 + off1)
+        for off2 in (0, 3, 1):
+            self.recv(self.buf.at[pl.ds(self.p.twin_group(off2), RING)], 16 + off2)
+        for off1 in (0, 3, 1, 2):
+            self.recv(self.buf.at[self.p.twin_index(2, off1)], 20 + off1)
 
     def finish(self):
         for copy in self.started:
@@ -143,7 +154,7 @@
     nq, s_own, x, nqp, wt, key_out, key_in, s_in, y_out, y_in, z_out, z_in, t_out, t_in, u_out, u_in, w_out, w_in,
     m_out, m_in, far_in,
     nq_hi, nq_lo, s_hl, p_hl, oh, gt, vt_hi, vt_lo, b_hi, b_lo, ws_hi, ws_lo, wn_hi, wn_lo,
-    k_hi, k_lo, x_hl, c_hl, st_hl,
+    k_hi, k_lo, x_hl, c_hl, st_hl, v_all,
     gsend, grecv, csend, crecv, osend, orecv, load_sem,
 ):
     leaf, cols = incident.shape
@@ -156,7 +167,7 @@
     near_tile, leaf_tile = near // 2, leaf // 2
     row_parts = (pl.ds(0, 2 * leaf // 3), pl.ds(2 * leaf // 3, leaf // 3))
     place = Place()
-    mine = place.col
+    mine = place.index(0, 0)
     started = []
 
     def lane(i):
@@ -271,8 +282,6 @@
 
     tiles(leaf, leaf_tile, last_far)
     far_swap = send(w_out, w_in, once, 3, place.cross)
-    make_one_hot(2, key_out, place.mate[0])
-    make_one_hot(0, key_out, place.leaf)
     own_partial(0)
     loads[8].wait()
 
@@ -286,50 +295,50 @@
 
         tiles(leaf, leaf_tile, body)
 
+    def split_swapped(i):
+        source_swaps[i].wait_recv()
+
+        def body(rows):
+            s_hl[i, rows, :] = beside(s_in[i, rows, :])
+
+        tiles(leaf, LANES, body)
+
     for g, swap in zip(near_gs, near_swaps):
         swap.wait_recv()
         g.ring1()
         g.ring2(0)
-        g.to_twin(0, 0)
-    own_partial(1)
-    own_sums(last)
+    make_one_hot(0, key_out, place.leaf)
+    own_sums(0)
+    make_one_hot(2, key_out, place.mate[0])
     for g in near_gs:
         for off1 in (3, 1, 2):
             g.ring1_recv(off1)
             g.ring2(off1)
         g.ring2_pass(0)
     for g in near_gs:
+        g.to_twin(0)
+    own_partial(1)
+    for g in near_gs:
         for off1 in (3, 1, 2):
-            g.to_twin(0, off1)
-    own_sums(0)
-    for i in range(2, last):
-        own_partial(i)
-    for off1 in (3, 1, 2):
-        near_gs[0].ring2_pass(off1)
-    own_sums(1)
-    for off1 in (3, 1, 2):
-        near_gs[1].ring2_pass(off1)
+            g.ring2_pass(off1)
     wt_g.ring2(0)
     for off1 in (3, 1, 2):
         wt_g.ring1_recv(off1)
         wt_g.ring2(off1)
     for g in near_gs:
-        for off1 in (0, 3, 1, 2):
-            g.to_twin(3, off1)
-            g.to_twin(1, off1)
+        g.to_twin(3)
+        g.to_twin(1)
     key_swap.wait_recv()
     make_one_hot(5, key_in, place.cross[0])
+    split_swapped(0)
+    for off1 in (0, 3, 1, 2):
+        near_gs[0].end_to_twin(off1)
+    for i in range(2, last):
+        own_partial(i)
+    for off1 in (0, 3, 1, 2):
+        near_gs[1].end_to_twin(off1)
     make_one_hot(4, key_in, place.leaf)
-    for off1 in (0, 3, 1, 2):
-        near_gs[0].ring2_end(off1)
-        near_gs[0].to_twin(2, off1)
-    for i in range(2, last):
-        own_sums(i)
-    for off1 in (0, 3, 1, 2):
-        near_gs[1].ring2_end(off1)
-        near_gs[1].to_twin(2, off1)
-    for off1 in (0, 3, 1, 2):
-        wt_g.to_twin(0, off1)
+    wt_g.to_twin(0)
 
     def split_partner(h):
         count = 4 * part
@@ -345,12 +354,8 @@
     z_swaps, t_swaps = {}, {}
 
     def near_chunk(i):
-        source_swaps[i].wait_recv()
-
-        def split(rows):
-            s_hl[i, rows, :] = beside(s_in[i, rows, :])
-
-        tiles(leaf, LANES, split)
+        if i > 0:
+            split_swapped(i)
         if i == 0:
             for h in range(2):
                 near_gs[h].from_twin()
@@ -378,19 +383,21 @@
         return send(u_out, u_in, once, 4, place.mate)
 
     def weights():
-        def split(index, carry):
-            count = 2 * inverse.shape[0]
-            rows = pl.ds(pl.multiple_of(index * count, 16), count)
-            both = wt[pl.ds(2 * index, 2), :, pl.ds(0, leaf + 4 * rank)]
-            ws_hi[rows, :], ws_lo[rows, :] = halves(both.reshape(count, leaf + 4 * rank))
+        count = inverse.shape[0]
+        scale = [1.0 / math.sqrt(2**k * leaf) for k in range(2)]
+
+        def split(pair, carry):
+            rows = pl.ds(pl.multiple_of(pair * 2 * count, 16), 2 * count)
+            other = RING * RING + (pair % RING) * RING + pair // RING
+            both = jnp.concatenate([wt[pair], wt[other]], axis=0)
+            ws_hi[rows, :], ws_lo[rows, :] = halves(both[:, : leaf + 4 * rank])
+            for k in range(2):
+                at = leaf + (4 + k) * rank
+                v_all[rows, pl.ds(k * rank, rank)] = both[:, at : at + rank] * scale[k]
             return carry
 
-        lax.fori_loop(0, wt.shape[0] // 2, split, 0)
-        for k in range(2):
-            v = wt[:, :, pl.ds(leaf + (4 + k) * rank, rank)].reshape(leaf, rank)
-            v = v * (1.0 / math.sqrt(2**k * leaf))
-            rows = pl.ds(k * rank, rank)
-            vt_hi[rows, :], vt_lo[rows, :] = halves(v.T)
+        lax.fori_loop(0, RING * RING, split, 0)
+        vt_hi[...], vt_lo[...] = halves(v_all[...].T)
         second_v = pl.ds(rank, rank)
         first_w = pl.ds(leaf, 2 * rank)
         m_out[...] = dot3(vt_hi[second_v, :], vt_lo[second_v, :], ws_hi[:, first_w], ws_lo[:, first_w])
@@ -494,18 +501,21 @@
     direct = last - 1
     far_swaps = []
     near_chunk(0)
+    own_sums(1)
+    wt_g.ring2_pass(0)
+    wt_g.ring2_pass(3)
     near_chunk(1)
+    wt_g.ring2_pass(1)
+    wt_g.ring2_pass(2)
+    own_sums(last)
     mate_sums = pass_on()
-    for off1 in (0, 3, 1, 2):
-        wt_g.ring2_pass(off1)
-    for off1 in (0, 3, 1, 2):
-        wt_g.to_twin(3, off1)
-        wt_g.to_twin(1, off1)
+    wt_g.to_twin(3)
+    wt_g.to_twin(1)
     for i in range(2, last):
+        own_sums(i)
         near_chunk(i)
     for off1 in (0, 3, 1, 2):
-        wt_g.ring2_end(off1)
-        wt_g.to_twin(2, off1)
+        wt_g.end_to_twin(off1)
     wt_g.from_twin()
     m_swap = weights()
     first(0)
@@ -518,25 +528,15 @@
     first(direct)
     for i in (0, last, 1):
         third(i)
-    at_once(direct)
-
+    final = [far_swaps[0], t_swaps[direct], z_swaps[direct]]
     for copy in started:
-        copy.wait_send()
+        if not any(copy is other for other in final):
+            copy.wait_send()
     for g in (*near_gs, wt_g):
         g.finish()
-
-
-def hand_over(value, out, out_sem):
-    count = out_sem.shape[0]
-    size = value.shape[0] // count
-    copies = [
-        pltpu.make_async_copy(value.at[pl.ds(i * size, size)], out.at[pl.ds(i * size, size)], out_sem.at[i])
-        for i in range(count)
-    ]
-    for copy in copies:
-        copy.start()
-    for copy in copies:
-        copy.wait()
+    at_once(direct)
+    for copy in final:
+        copy.wait_send()
 
 
 def per_device(
@@ -573,12 +573,12 @@
         *pair(2 * rank, leaf), *pair(2 * rank, leaf),
         *pair(leaf, leaf + 4 * rank), *pair(leaf, 4 * rank),
         *pair(rank, 2 * rank), vmem((leaf, 2 * LANES), BF16), vmem((4 * rank, 2 * LANES), BF16),
-        vmem((leaf, 2 * LANES), BF16),
+        vmem((leaf, 2 * LANES), BF16), f32(leaf, 2 * rank),
         sem((3, 32)), sem((3, 32)), sem((5, chunks)), sem((5, chunks)), sem((8,)), sem((8,)),
         sem((9,)),
     ]
     in_any = pl.BlockSpec(memory_space=pl.ANY)
-    solved = pl.pallas_call(
+    return pl.pallas_call(
         kernel,
         out_shape=pltpu.VMEM((leaf, cols), F32),
         in_specs=[in_any] * 9,
@@ -592,14 +592,6 @@
         tree_order, near_owner.reshape(1, near), near_slot.reshape(1, near),
         leaf_inverse, basis_v, basis_w, incident, sources, near_quad,
     )
-    return pl.pallas_call(
-        hand_over,
-        out_shape=jax.ShapeDtypeStruct((leaf, cols), F32),
-        in_specs=[pl.BlockSpec(memory_space=pltpu.VMEM)],
-        out_specs=in_any,
-        scratch_shapes=[sem((chunks,))],
-    )(solved)
-
 
 def solution(mesh):
     placed = (

time: 73 us -> 69.9 us (0.958)
  Pallas kernels: 70.8 us -> 68 us
    pallas_call x1 -> x0, Pallas kernels: 2.57 us -> none  [per_device(): pl.pallas_call(hand_over, out_shape=jax.ShapeDtypeStruct((leaf, cols), F3...]
where the time goes in v5:
time: 69.9 us; the launch traced here: 69.2 us
  Pallas kernels  68 us (97%)
  local copies, waits for them, and re-layouts  1.15 us (2%)
    pallas_call x1, Pallas kernels, per_device(): pl.pallas_call(kernel, out_shape=pltpu.VMEM((leaf, cols), F32), in_specs=...  68 us

profile of v5, /device:TPU:0, one launch (start us, length us, event | category | flops | bytes accessed | tf_op | source)
XLA Modules:
  0.0 69.2 jit_solution(12244848334053650326)
XLA Ops:
  0.0 68.0 %shard_map.91 = f32[768,512]{1,0:T(8,128)S(1)} custom-call(s32[1,768]{1,0:T(1,128)} %tree_any.1, s32[1,1024]{1,0:T(1,128)} %bitcast.2, s32[1,1024]{1,0:T(1,128)} %bitcast.3, f32[24,768]{1,0:T(8,128)} %inverse_any.1, f32[2,24,128]{2,1,0:T(8,128)} %basis_v_any.1, f32[2,2,24,128]{3,2,1,0:T(8,128)} %basis_w_any.1, f32[768,512]{1,0:T(8,128)} %incident.1, ...), custom_call_target="tpu_custom_call" | custom-call | flops 15000000512 | bytes 12000000 | tf_op jit(solution)/shard_map/pallas_call | solution.py:581
  68.0 1.1 %copy.11 = f32[768,512]{1,0:T(8,128)} copy(f32[768,512]{1,0:T(8,128)S(1)} %shard_map.91) | data formatting | bytes 3145728

commit v6 on v5

--- a/solution.py
+++ b/solution.py
@@ -249,8 +249,6 @@
     make_one_hot(3, key_out, place.far[0])
     loads[6].wait()
     tiles(near, LANES, split_near)
-    loads[7].wait()
-    own_partial(last)
 
     pl.semaphore_wait(barrier, len(neighbours))
 
@@ -272,6 +270,8 @@
         rows = row_parts[part]
         return send(y_out.at[i, rows], y_in.at[i, rows], per, (1 + 3 * part, i), place.cross)
 
+    loads[7].wait()
+    own_partial(last)
     sum_swaps = {last: []}
     for k in range(2):
         y_out[last, row_parts[k], :] = sums(1, last, row_parts[k])
@@ -282,7 +282,8 @@
 
     tiles(leaf, leaf_tile, last_far)
     far_swap = send(w_out, w_in, once, 3, place.cross)
-    own_partial(0)
+    make_one_hot(0, key_out, place.leaf)
+    make_one_hot(2, key_out, place.mate[0])
     loads[8].wait()
 
     def own_sums(i):
@@ -307,9 +308,8 @@
         swap.wait_recv()
         g.ring1()
         g.ring2(0)
-    make_one_hot(0, key_out, place.leaf)
+    own_partial(0)
     own_sums(0)
-    make_one_hot(2, key_out, place.mate[0])
     for g in near_gs:
         for off1 in (3, 1, 2):
             g.ring1_recv(off1)
@@ -337,7 +337,6 @@
         own_partial(i)
     for off1 in (0, 3, 1, 2):
         near_gs[1].end_to_twin(off1)
-    make_one_hot(4, key_in, place.leaf)
     wt_g.to_twin(0)
 
     def split_partner(h):
@@ -357,16 +356,25 @@
         if i > 0:
             split_swapped(i)
         if i == 0:
+            span = [pl.ds(h * near // 2, near // 2) for h in range(2)]
             for h in range(2):
                 near_gs[h].from_twin()
                 split_partner(h)
-                partial_rows(i, pl.ds(h * near // 2, near // 2))
+                partial_rows(i, span[h])
+                if h == 0:
+                    for rows in row_parts:
+                        y_out[i, rows, :] += fold(dot(oh[5, rows, span[0]], p_hl[i, span[0], :]))
         else:
             partial(i)
         sum_swaps[i] = []
-        for k in range(2):
-            y_out[i, row_parts[k], :] += sums(5, i, row_parts[k])
+        for k, rows in enumerate(row_parts):
+            if i == 0:
+                y_out[i, rows, :] += fold(dot(oh[5, rows, span[1]], p_hl[i, span[1], :]))
+            else:
+                y_out[i, rows, :] += sums(5, i, rows)
             sum_swaps[i].append(send_sums(i, k))
+        if i == 0:
+            make_one_hot(4, key_in, place.leaf)
 
         def here(rows):
             x[rows, lane(i)] += sums(4, i, rows)

time: 69.9 us -> 68 us (0.973)
  Pallas kernels: 68 us -> 66.1 us
    pallas_call x1, Pallas kernels: 68 us -> 66.1 us  [per_device(): pl.pallas_call(kernel, out_shape=pltpu.VMEM((leaf, cols), F32), in_specs=...]
where the time goes in v6:
time: 68 us; the launch traced here: 67.3 us
  Pallas kernels  66.1 us (97%)
  local copies, waits for them, and re-layouts  1.15 us (2%)
    pallas_call x1, Pallas kernels, per_device(): pl.pallas_call(kernel, out_shape=pltpu.VMEM((leaf, cols), F32), in_specs=...  66.1 us

profile of v6, /device:TPU:0, one launch (start us, length us, event | category | flops | bytes accessed | tf_op | source)
XLA Modules:
  0.0 67.3 jit_solution(16550437011999793928)
XLA Ops:
  0.0 66.1 %shard_map.91 = f32[768,512]{1,0:T(8,128)S(1)} custom-call(s32[1,768]{1,0:T(1,128)} %tree_any.1, s32[1,1024]{1,0:T(1,128)} %bitcast.2, s32[1,1024]{1,0:T(1,128)} %bitcast.3, f32[24,768]{1,0:T(8,128)} %inverse_any.1, f32[2,24,128]{2,1,0:T(8,128)} %basis_v_any.1, f32[2,2,24,128]{3,2,1,0:T(8,128)} %basis_w_any.1, f32[768,512]{1,0:T(8,128)} %incident.1, ...), custom_call_target="tpu_custom_call" | custom-call | flops 15000000512 | bytes 12000000 | tf_op jit(solution)/shard_map/pallas_call | solution.py:589
  66.1 1.1 %copy.11 = f32[768,512]{1,0:T(8,128)} copy(f32[768,512]{1,0:T(8,128)S(1)} %shard_map.91) | data formatting | bytes 3145728

commit v7 on v6

--- a/solution.py
+++ b/solution.py
@@ -151,7 +151,7 @@
 def kernel(
     tree_any, owner_any, slot_any, inverse_any, basis_v_any, basis_w_any, incident, sources, near_quad, nat,
     tree, owner, slot, inverse, basis_v, basis_w,
-    nq, s_own, x, nqp, wt, key_out, key_in, s_in, y_out, y_in, z_out, z_in, t_out, t_in, u_out, u_in, w_out, w_in,
+    nq, s_own, x, nqp_first, nqp_second, wt, key_out, key_in, s_in, y_out, y_in, z_out, z_in, t_out, t_in, u_out, u_in, w_out, w_in,
     m_out, m_in, far_in,
     nq_hi, nq_lo, s_hl, p_hl, oh, gt, vt_hi, vt_lo, b_hi, b_lo, ws_hi, ws_lo, wn_hi, wn_lo,
     k_hi, k_lo, x_hl, c_hl, st_hl, v_all,
@@ -160,8 +160,10 @@
     leaf, cols = incident.shape
     near = near_quad.shape[0]
     rank = basis_v.shape[2]
-    part = nqp.shape[2]
-    group = nqp.shape[1]
+    nqp = (nqp_first, nqp_second)
+    group = nqp_first.shape[0]
+    cut = group * nqp_first.shape[1]
+    span = [pl.ds(0, cut), pl.ds(cut, near - cut)]
     chunks = cols // LANES
     last = chunks - 1
     near_tile, leaf_tile = near // 2, leaf // 2
@@ -173,9 +175,11 @@
     def lane(i):
         return pl.ds(i * LANES, LANES)
 
+    others = pl.ds(0, last * LANES)
     pairs = (
         (tree_any, tree), (owner_any, owner), (slot_any, slot), (inverse_any, inverse), (basis_v_any, basis_v),
-        (basis_w_any, basis_w), (near_quad, nq), (sources, s_own), (incident, x),
+        (basis_w_any, basis_w), (near_quad, nq), (sources.at[:, lane(last)], s_own.at[:, lane(last)]), (incident, x),
+        (sources.at[:, others], s_own.at[:, others]),
     )
     loads = [pltpu.make_async_copy(src, dst, load_sem.at[i]) for i, (src, dst) in enumerate(pairs)]
     barrier = pltpu.get_barrier_semaphore()
@@ -185,7 +189,7 @@
     )
     for device in neighbours:
         pl.semaphore_signal(barrier, inc=1, device_id=device, device_id_type=MESH)
-    for copy in loads:
+    for copy in loads[:8]:
         copy.start()
 
     def send(src, dst, sems, index, device):
@@ -197,7 +201,7 @@
         started.append(copy)
         return copy
 
-    near_gs = [Gather(place, nqp.at[h], gsend.at[h], grecv.at[h]) for h in range(2)]
+    near_gs = [Gather(place, nqp[h], gsend.at[h], grecv.at[h]) for h in range(2)]
     wt_g = Gather(place, wt, gsend.at[2], grecv.at[2])
 
     def make_gt(rows):
@@ -245,17 +249,14 @@
         wt[mine, :, pl.ds(leaf + k * rank, rank)] = basis_w[k // 2, k % 2]
     for k in range(2):
         wt[mine, :, pl.ds(leaf + (4 + k) * rank, rank)] = basis_v[k]
-    make_one_hot(1, key_out, place.cross[0])
-    make_one_hot(3, key_out, place.far[0])
-    loads[6].wait()
-    tiles(near, LANES, split_near)
 
     pl.semaphore_wait(barrier, len(neighbours))
 
     once, per = (osend, orecv), (csend, crecv)
     near_swaps = [
         send(
-            near_quad.at[pl.ds(pl.multiple_of(h * near // 2 + mine * part, part), part)], nqp.at[h, mine],
+            near_quad.at[pl.ds(pl.multiple_of(h * cut + mine * nqp[h].shape[1], 8), nqp[h].shape[1])],
+            nqp[h].at[mine],
             once, h, place.mate,
         )
         for h in range(2)
@@ -270,12 +271,19 @@
         rows = row_parts[part]
         return send(y_out.at[i, rows], y_in.at[i, rows], per, (1 + 3 * part, i), place.cross)
 
+    for copy in loads[8:]:
+        copy.start()
+    loads[6].wait()
+    tiles(near, LANES, split_near)
     loads[7].wait()
     own_partial(last)
+    make_one_hot(1, key_out, place.cross[0])
     sum_swaps = {last: []}
     for k in range(2):
         y_out[last, row_parts[k], :] = sums(1, last, row_parts[k])
         sum_swaps[last].append(send_sums(last, k))
+
+    make_one_hot(3, key_out, place.far[0])
 
     def last_far(rows):
         w_out[rows, :] = sums(3, last, rows)
@@ -285,6 +293,7 @@
     make_one_hot(0, key_out, place.leaf)
     make_one_hot(2, key_out, place.mate[0])
     loads[8].wait()
+    loads[9].wait()
 
     def own_sums(i):
         def body(rows):
@@ -340,11 +349,11 @@
     wt_g.to_twin(0)
 
     def split_partner(h):
-        count = 4 * part
+        count = 4 * nqp[h].shape[1]
 
         def body(index, carry):
-            rows = pl.ds(pl.multiple_of(h * near // 2 + index * count, count), count)
-            block = nqp[h, pl.ds(4 * index, 4)].reshape(count, leaf)
+            rows = pl.ds(pl.multiple_of(h * cut + index * count, count), count)
+            block = nqp[h][pl.ds(4 * index, 4)].reshape(count, leaf)
             nq_hi[rows, :], nq_lo[rows, :] = halves(block)
             return carry
 
@@ -356,7 +365,6 @@
         if i > 0:
             split_swapped(i)
         if i == 0:
-            span = [pl.ds(h * near // 2, near // 2) for h in range(2)]
             for h in range(2):
                 near_gs[h].from_twin()
                 split_partner(h)
@@ -459,11 +467,14 @@
             z = term if z is None else z + term
         z_out[i] = z
         if i == direct:
+            own_swaps.append(send(z_out.at[i, one], z_in.at[i, one], once, 8, place.mate))
             own = beside(z_out[i, one, :])
             z_out[i, two, :] = z_out[i, two, :] - dot_beside(k_hi[:, two], k_lo[:, two], own)
-            far_swaps.append(send(z_out.at[i, two], far_in, once, 7, place.far))
-            t_swaps[i] = send(z_out.at[i, two], t_in.at[i], per, (3, i), place.cross)
-        z_swaps[i] = send(z_out.at[i], z_in.at[i], per, (2, i), place.mate)
+            own_swaps.append(send(z_out.at[i, two], far_in, once, 7, place.far))
+            own_swaps.append(send(z_out.at[i, two], t_in.at[i], per, (3, i), place.cross))
+            own_swaps.append(send(z_out.at[i, two], z_in.at[i, two], per, (2, i), place.mate))
+        else:
+            z_swaps[i] = send(z_out.at[i], z_in.at[i], per, (2, i), place.mate)
 
         def state(rows):
             st_hl[rows, :] = beside(dot_beside(ws_hi[rows, state_columns], ws_lo[rows, state_columns], x_hl[...]))
@@ -497,17 +508,16 @@
         tiles(leaf, leaf_tile, lambda rows: correct(rows, i, 2, 1))
 
     def at_once(i):
-        z_swaps[i].wait_recv()
+        for copy in own_swaps:
+            copy.wait_recv()
         c_hl[one, :] = beside(z_in[i, one, :])
         c_hl[two, :] = beside(z_out[i, one, :])
+        c_hl[pl.ds(2 * rank, rank), :] = beside(t_in[i] + far_in[...])
         c_hl[pl.ds(3 * rank, rank), :] = beside(z_out[i, two, :] + z_in[i, two, :])
-        t_swaps[i].wait_recv()
-        far_swaps[0].wait_recv()
-        c_hl[pl.ds(2 * rank, rank), :] = beside(t_in[i] + far_in[...])
         tiles(leaf, leaf_tile, lambda rows: correct(rows, i, 0, 4))
 
     direct = last - 1
-    far_swaps = []
+    own_swaps = []
     near_chunk(0)
     own_sums(1)
     wt_g.ring2_pass(0)
@@ -536,14 +546,13 @@
     first(direct)
     for i in (0, last, 1):
         third(i)
-    final = [far_swaps[0], t_swaps[direct], z_swaps[direct]]
     for copy in started:
-        if not any(copy is other for other in final):
+        if not any(copy is other for other in own_swaps):
             copy.wait_send()
     for g in (*near_gs, wt_g):
         g.finish()
     at_once(direct)
-    for copy in final:
+    for copy in own_swaps:
         copy.wait_send()
 
 
@@ -569,7 +578,7 @@
         vmem((1, leaf), jnp.int32), vmem((1, near), jnp.int32), vmem((1, near), jnp.int32),
         f32(rows, leaf), f32(2, rows, rank), f32(2, 2, rows, rank),
         f32(near, leaf), f32(leaf, cols), f32(leaf, cols),
-        f32(2, group, near // (2 * group), leaf), f32(group, rows, width),
+        f32(group, 3 * near // (4 * group), leaf), f32(group, near // (4 * group), leaf), f32(group, rows, width),
         vmem((1, near), jnp.int32), vmem((1, near), jnp.int32),
         f32(chunks, leaf, LANES), f32(chunks, leaf, LANES), f32(chunks, leaf, LANES),
         f32(chunks, 2 * rank, LANES), f32(chunks, 2 * rank, LANES),
@@ -582,8 +591,8 @@
         *pair(leaf, leaf + 4 * rank), *pair(leaf, 4 * rank),
         *pair(rank, 2 * rank), vmem((leaf, 2 * LANES), BF16), vmem((4 * rank, 2 * LANES), BF16),
         vmem((leaf, 2 * LANES), BF16), f32(leaf, 2 * rank),
-        sem((3, 32)), sem((3, 32)), sem((5, chunks)), sem((5, chunks)), sem((8,)), sem((8,)),
-        sem((9,)),
+        sem((3, 32)), sem((3, 32)), sem((5, chunks)), sem((5, chunks)), sem((9,)), sem((9,)),
+        sem((10,)),
     ]
     in_any = pl.BlockSpec(memory_space=pl.ANY)
     return pl.pallas_call(

time: 68 us -> 68.4 us (level)
  Pallas kernels: 66.1 us -> 67.1 us
    pallas_call x1, Pallas kernels: 66.1 us -> 67.1 us  [per_device(): pl.pallas_call(kernel, out_shape=pltpu.VMEM((leaf, cols), F32), in_specs=...]
where the time goes in v7:
time: 68.4 us; the launch traced here: 68.3 us
  Pallas kernels  67.1 us (98%)
  local copies, waits for them, and re-layouts  1.15 us (2%)
    pallas_call x1, Pallas kernels, per_device(): pl.pallas_call(kernel, out_shape=pltpu.VMEM((leaf, cols), F32), in_specs=...  67.1 us

profile of v7, /device:TPU:0, one launch (start us, length us, event | category | flops | bytes accessed | tf_op | source)
XLA Modules:
  0.0 68.3 jit_solution(6625451041677624921)
XLA Ops:
  0.0 67.1 %shard_map.91 = f32[768,512]{1,0:T(8,128)S(1)} custom-call(s32[1,768]{1,0:T(1,128)} %tree_any.1, s32[1,1024]{1,0:T(1,128)} %bitcast.2, s32[1,1024]{1,0:T(1,128)} %bitcast.3, f32[24,768]{1,0:T(8,128)} %inverse_any.1, f32[2,24,128]{2,1,0:T(8,128)} %basis_v_any.1, f32[2,2,24,128]{3,2,1,0:T(8,128)} %basis_w_any.1, f32[768,512]{1,0:T(8,128)} %incident.1, ...), custom_call_target="tpu_custom_call" | custom-call | flops 15000000512 | bytes 12000000 | tf_op jit(solution)/shard_map/pallas_call | solution.py:598
  67.1 1.1 %copy.11 = f32[768,512]{1,0:T(8,128)} copy(f32[768,512]{1,0:T(8,128)S(1)} %shard_map.91) | data formatting | bytes 3145728

commit v8 on v7

--- a/solution.py
+++ b/solution.py
@@ -151,7 +151,7 @@
 def kernel(
     tree_any, owner_any, slot_any, inverse_any, basis_v_any, basis_w_any, incident, sources, near_quad, nat,
     tree, owner, slot, inverse, basis_v, basis_w,
-    nq, s_own, x, nqp_first, nqp_second, wt, key_out, key_in, s_in, y_out, y_in, z_out, z_in, t_out, t_in, u_out, u_in, w_out, w_in,
+    nq, s_own, x, nqp, wt, key_out, key_in, s_in, y_out, y_in, z_out, z_in, t_out, t_in, u_out, u_in, w_out, w_in,
     m_out, m_in, far_in,
     nq_hi, nq_lo, s_hl, p_hl, oh, gt, vt_hi, vt_lo, b_hi, b_lo, ws_hi, ws_lo, wn_hi, wn_lo,
     k_hi, k_lo, x_hl, c_hl, st_hl, v_all,
@@ -160,10 +160,8 @@
     leaf, cols = incident.shape
     near = near_quad.shape[0]
     rank = basis_v.shape[2]
-    nqp = (nqp_first, nqp_second)
-    group = nqp_first.shape[0]
-    cut = group * nqp_first.shape[1]
-    span = [pl.ds(0, cut), pl.ds(cut, near - cut)]
+    part = nqp.shape[2]
+    group = nqp.shape[1]
     chunks = cols // LANES
     last = chunks - 1
     near_tile, leaf_tile = near // 2, leaf // 2
@@ -201,7 +199,7 @@
         started.append(copy)
         return copy
 
-    near_gs = [Gather(place, nqp[h], gsend.at[h], grecv.at[h]) for h in range(2)]
+    near_gs = [Gather(place, nqp.at[h], gsend.at[h], grecv.at[h]) for h in range(2)]
     wt_g = Gather(place, wt, gsend.at[2], grecv.at[2])
 
     def make_gt(rows):
@@ -255,8 +253,7 @@
     once, per = (osend, orecv), (csend, crecv)
     near_swaps = [
         send(
-            near_quad.at[pl.ds(pl.multiple_of(h * cut + mine * nqp[h].shape[1], 8), nqp[h].shape[1])],
-            nqp[h].at[mine],
+            near_quad.at[pl.ds(pl.multiple_of(h * near // 2 + mine * part, part), part)], nqp.at[h, mine],
             once, h, place.mate,
         )
         for h in range(2)
@@ -349,11 +346,11 @@
     wt_g.to_twin(0)
 
     def split_partner(h):
-        count = 4 * nqp[h].shape[1]
+        count = 4 * part
 
         def body(index, carry):
-            rows = pl.ds(pl.multiple_of(h * cut + index * count, count), count)
-            block = nqp[h][pl.ds(4 * index, 4)].reshape(count, leaf)
+            rows = pl.ds(pl.multiple_of(h * near // 2 + index * count, count), count)
+            block = nqp[h, pl.ds(4 * index, 4)].reshape(count, leaf)
             nq_hi[rows, :], nq_lo[rows, :] = halves(block)
             return carry
 
@@ -365,6 +362,7 @@
         if i > 0:
             split_swapped(i)
         if i == 0:
+            span = [pl.ds(h * near // 2, near // 2) for h in range(2)]
             for h in range(2):
                 near_gs[h].from_twin()
                 split_partner(h)
@@ -578,7 +576,7 @@
         vmem((1, leaf), jnp.int32), vmem((1, near), jnp.int32), vmem((1, near), jnp.int32),
         f32(rows, leaf), f32(2, rows, rank), f32(2, 2, rows, rank),
         f32(near, leaf), f32(leaf, cols), f32(leaf, cols),
-        f32(group, 3 * near // (4 * group), leaf), f32(group, near // (4 * group), leaf), f32(group, rows, width),
+        f32(2, group, near // (2 * group), leaf), f32(group, rows, width),
         vmem((1, near), jnp.int32), vmem((1, near), jnp.int32),
         f32(chunks, leaf, LANES), f32(chunks, leaf, LANES), f32(chunks, leaf, LANES),
         f32(chunks, 2 * rank, LANES), f32(chunks, 2 * rank, LANES),

time: 68.4 us -> 68 us (level)
  no operation moved by 1% of the time
where the time goes in v8:
time: 68 us; the launch traced here: 67.9 us
  Pallas kernels  66.7 us (98%)
  local copies, waits for them, and re-layouts  1.15 us (2%)
    pallas_call x1, Pallas kernels, per_device(): pl.pallas_call(kernel, out_shape=pltpu.VMEM((leaf, cols), F32), in_specs=...  66.7 us

profile of v8, /device:TPU:0, one launch (start us, length us, event | category | flops | bytes accessed | tf_op | source)
XLA Modules:
  0.0 67.9 jit_solution(15706196473841797089)
XLA Ops:
  0.0 66.7 %shard_map.91 = f32[768,512]{1,0:T(8,128)S(1)} custom-call(s32[1,768]{1,0:T(1,128)} %tree_any.1, s32[1,1024]{1,0:T(1,128)} %bitcast.2, s32[1,1024]{1,0:T(1,128)} %bitcast.3, f32[24,768]{1,0:T(8,128)} %inverse_any.1, f32[2,24,128]{2,1,0:T(8,128)} %basis_v_any.1, f32[2,2,24,128]{3,2,1,0:T(8,128)} %basis_w_any.1, f32[768,512]{1,0:T(8,128)} %incident.1, ...), custom_call_target="tpu_custom_call" | custom-call | flops 15000000512 | bytes 12000000 | tf_op jit(solution)/shard_map/pallas_call | solution.py:596
  66.7 1.1 %copy.11 = f32[768,512]{1,0:T(8,128)} copy(f32[768,512]{1,0:T(8,128)S(1)} %shard_map.91) | data formatting | bytes 3145728
